TPU v7x, 32 devices: a whole 2x2x4 slice. The times are simulated.
32 devices in a mesh: dp: 8 (over z, y), task: 4 (over x, core).
Axes of the slice: x: 2, y: 2, z: 4, core: 2. Of those that a mesh axis runs over, the one named last changes fastest.
Arguments:
- inputs: bfloat16 [8, 32, 48, 512], P('dp', None, None, 'task'), may hold values from -18 to 18
- extents: int32 [8, 2], P('dp'), may hold values from 1 to 48, as said below
- conflicts: int32 [4, 4], replicated, may hold values 0 or 1
- trunk_weight: float32 [9, 512, 512], P(None, 'dp', 'task'), may hold values from -0.09375 to 0.09375
- attn_first: float32 [4, 512, 512], P('task', 'dp'), may hold values from -0.25 to 0.25
- attn_second: float32 [4, 512, 512], P('task', 'dp'), may hold values from -0.25 to 0.25
- branch_conv: float32 [4, 9, 512, 512], P('task', None, 'dp'), may hold values from -0.09375 to 0.09375
- trunk_momentum: float32 [9, 512, 512], P(None, 'dp', 'task'), may hold values from -64 to 64
- first_momentum: float32 [4, 512, 512], P('task', 'dp'), may hold values from -64 to 64
- second_momentum: float32 [4, 512, 512], P('task', 'dp'), may hold values from -64 to 64
- conv_momentum: float32 [4, 9, 512, 512], P('task', None, 'dp'), may hold values from -64 to 64
- cotangent: bfloat16 [4, 8, 16, 24, 512], P('task', 'dp'), may hold values from -6 to 6
Outputs:
- features: bfloat16 [4, 8, 16, 24, 512], P('task', 'dp')
- input_grad: float32 [8, 32, 48, 512], P('dp', None, None, 'task')
- trunk_weight_new: float32 [9, 512, 512], P(None, 'dp', 'task')
- attn_first_new: float32 [4, 512, 512], P('task', 'dp')
- attn_second_new: float32 [4, 512, 512], P('task', 'dp')
- branch_conv_new: float32 [4, 9, 512, 512], P('task', None, 'dp')
- trunk_momentum_new: float32 [9, 512, 512], P(None, 'dp', 'task')
- first_momentum_new: float32 [4, 512, 512], P('task', 'dp')
- second_momentum_new: float32 [4, 512, 512], P('task', 'dp')
- conv_momentum_new: float32 [4, 9, 512, 512], P('task', None, 'dp')
- task_gram: float32 [4, 4], replicated
Inputs may be any that keep to these rules, and one draw needn't show every extreme that they name: Image i's valid pixels are its rows below extents[i, 0] and its columns below extents[i, 1]; extents[i, 0] <= 32 and extents[i, 1] <= 48.
All inputs are finite; a program needn't handle non-finite values.
Results may differ from a plain program's by a relative error of at most 0.0095.
Values may be sent and summed in bfloat16 or wider, within the bound.
No kernel may reach another device: no remote copies, remote signals or barrier semaphores. Data moves between devices by JAX's collectives and lax.ppermute only.
A program may use at most 192 MiB of HBM per device.

v0:
```python
import jax
import jax.numpy as jnp
from jax import lax
from jax.sharding import PartitionSpec as P

NS_STEPS = 3


epsilon = 1e-05
moment_decay = 0.95
step_rate = 1.0
weight_decay = 0.01
coeff_a = 3.4445
coeff_b = -4.775
coeff_c = 2.0315
highest = lax.Precision.HIGHEST


def conv_forward(values, kernel):
    height, across = (values.shape[1], values.shape[2])
    padded = jnp.pad(values, ((0, 0), (1, 1), (1, 1), (0, 0)))
    running = jnp.zeros(values.shape[:3] + (kernel.shape[2],), jnp.float32)
    for offset in range(9):
        row_off, col_off = (offset // 3, offset % 3)
        window = padded[:, row_off : row_off + height, col_off : col_off + across]
        running = running + jnp.einsum(
            "ihwc,co->ihwo", window, kernel[offset], preferred_element_type=jnp.float32
        )
    return running


def input_grads(grads, kernel, spec):
    height, across = (grads.shape[-3], grads.shape[-2])
    padding = [(0, 0)] * (grads.ndim - 3) + [(1, 1), (1, 1), (0, 0)]
    padded = jnp.pad(grads, padding)
    running = None
    for offset in range(9):
        row_off, col_off = (2 - offset // 3, 2 - offset % 3)
        window = padded[..., row_off : row_off + height, col_off : col_off + across, :]
        term = jnp.einsum(spec, window, kernel[offset], preferred_element_type=jnp.float32)
        running = term if running is None else running + term
    return running


def kernel_grads(values, grads, spec, stack_axis):
    height, across = (values.shape[1], values.shape[2])
    padded = jnp.pad(values, ((0, 0), (1, 1), (1, 1), (0, 0)))
    pieces = []
    for offset in range(9):
        row_off, col_off = (offset // 3, offset % 3)
        window = padded[:, row_off : row_off + height, col_off : col_off + across]
        pieces.append(jnp.einsum(spec, window, grads, preferred_element_type=jnp.float32))
    return jnp.stack(pieces, axis=stack_axis)


def norm_forward(values, mask, valid_count, local_extra):
    first_sum, second_sum, extra_total = lax.psum(
        (
            jnp.sum(values * mask, axis=(0, 1, 2)),
            jnp.sum(values * values * mask, axis=(0, 1, 2)),
            local_extra,
        ),
        "dp",
    )
    if valid_count is None:
        valid_count = extra_total
    average = first_sum / valid_count
    spread = second_sum / valid_count - average * average
    inverse_std = lax.rsqrt(spread + epsilon)
    return ((values - average) * inverse_std, inverse_std, valid_count)


def norm_backward(grad_norm, normed, inverse_std, mask, valid_count):
    first_sum, second_sum = lax.psum(
        (
            jnp.sum(grad_norm, axis=(-4, -3, -2), keepdims=True),
            jnp.sum(grad_norm * normed, axis=(-4, -3, -2), keepdims=True),
        ),
        "dp",
    )
    return inverse_std * (
        grad_norm - mask * first_sum / valid_count - mask * normed * second_sum / valid_count
    )


def silu_slope(values):
    sigma = jax.nn.sigmoid(values)
    return sigma * (1.0 + values * (1.0 - sigma))


def pcgrad_weights(task_gram, flags):
    count_tasks = task_gram.shape[0]
    identity_rows = jnp.eye(count_tasks, dtype=jnp.float32)
    combined = jnp.zeros((count_tasks,), jnp.float32)
    for target in range(count_tasks):
        coeffs = identity_rows[target]
        for source in range(count_tasks):
            if source != target:
                inner_prod = jnp.sum(coeffs * task_gram[:, source])
                coeffs = (
                    coeffs
                    - flags[target, source].astype(jnp.float32)
                    * inner_prod
                    / task_gram[source, source]
                    * identity_rows[source]
                )
        combined = combined + coeffs
    return combined


def gram_local(ortho):
    return jnp.einsum("kio,kip->op", ortho, ortho, precision=highest)


def ns_update(ortho, gram):
    combo = coeff_b * gram + coeff_c * jnp.dot(gram, gram, precision=highest)
    return coeff_a * ortho + jnp.einsum("kip,po->kio", ortho, combo, precision=highest)


def body(
    inputs,
    extents,
    conflicts,
    trunk_weight,
    attn_first,
    attn_second,
    branch_conv,
    trunk_momentum,
    first_momentum,
    second_momentum,
    conv_momentum,
    cotangent,
):
    images, height, across = (inputs.shape[0], inputs.shape[1], inputs.shape[2])
    rows_h = lax.broadcasted_iota(jnp.int32, (images, height, across), 1)
    cols_w = lax.broadcasted_iota(jnp.int32, (images, height, across), 2)
    mask = (
        (rows_h < extents[:, 0][:, None, None]) & (cols_w < extents[:, 1][:, None, None])
    ).astype(jnp.float32)[..., None]
    masked_part = (inputs.astype(jnp.float32) * mask).astype(jnp.bfloat16)
    full_in = lax.all_gather(masked_part, "task", axis=3, tiled=True)
    trunk_full, first_full, second_full, conv_full = (
        lax.all_gather(trunk_weight.astype(jnp.bfloat16), "dp", axis=1, tiled=True),
        lax.all_gather(attn_first[0].astype(jnp.bfloat16), "dp", axis=0, tiled=True),
        lax.all_gather(attn_second[0].astype(jnp.bfloat16), "dp", axis=0, tiled=True),
        lax.all_gather(branch_conv[0].astype(jnp.bfloat16), "dp", axis=1, tiled=True),
    )
    trunk_pre = conv_forward(full_in, trunk_full)
    trunk_norm, trunk_inv, valid_count = norm_forward(trunk_pre, mask, None, jnp.sum(mask))
    shared_part = (mask * jax.nn.silu(trunk_norm)).astype(jnp.bfloat16)
    shared = lax.all_gather(shared_part, "task", axis=3, tiled=True)
    first_pre = jnp.einsum("ihwc,co->ihwo", shared, first_full, preferred_element_type=jnp.float32)
    first_norm, first_inv = norm_forward(first_pre, mask, valid_count, jnp.float32(0.0))[:2]
    hidden = (mask * jax.nn.silu(first_norm)).astype(jnp.bfloat16)
    second_pre = jnp.einsum(
        "ihwc,co->ihwo", hidden, second_full, preferred_element_type=jnp.float32
    )
    second_norm, second_inv = norm_forward(second_pre, mask, valid_count, jnp.float32(0.0))[:2]
    gating = jax.nn.sigmoid(second_norm)
    shared_wide = shared.astype(jnp.float32)
    merged = (gating * shared_wide).astype(jnp.bfloat16)
    conv_pre = conv_forward(merged, conv_full)
    conv_norm, conv_inv = norm_forward(conv_pre, mask, valid_count, jnp.float32(0.0))[:2]
    activ = mask * jax.nn.silu(conv_norm)
    channels = activ.shape[3]
    pooled = activ.reshape(images, height // 2, 2, across // 2, 2, channels).mean(axis=(2, 4))
    features = pooled.astype(jnp.bfloat16)[None]
    upstream = cotangent[0].astype(jnp.float32)
    grad_act = jnp.repeat(jnp.repeat(upstream, 2, axis=1), 2, axis=2) * 0.25
    conv_grad = norm_backward(
        grad_act * mask * silu_slope(conv_norm), conv_norm, conv_inv, mask, valid_count
    ).astype(jnp.bfloat16)
    conv_kgrad = kernel_grads(merged, conv_grad, "ihwc,ihwo->co", 0)
    merged_grad = input_grads(conv_grad, jnp.swapaxes(conv_full, 1, 2), "ihwo,oc->ihwc")
    gate_grad = merged_grad * shared_wide
    shared_grad = merged_grad * gating
    second_grad = norm_backward(
        gate_grad * gating * (1.0 - gating), second_norm, second_inv, mask, valid_count
    ).astype(jnp.bfloat16)
    second_kgrad = jnp.einsum(
        "ihwc,ihwo->co", hidden, second_grad, preferred_element_type=jnp.float32
    )
    hidden_grad = jnp.einsum(
        "ihwo,co->ihwc", second_grad, second_full, preferred_element_type=jnp.float32
    )
    first_grad = norm_backward(
        hidden_grad * mask * silu_slope(first_norm), first_norm, first_inv, mask, valid_count
    ).astype(jnp.bfloat16)
    first_kgrad = jnp.einsum(
        "ihwc,ihwo->co", shared, first_grad, preferred_element_type=jnp.float32
    )
    shared_grad = shared_grad + jnp.einsum(
        "ihwo,co->ihwc", first_grad, first_full, preferred_element_type=jnp.float32
    )
    routed = lax.all_to_all(
        shared_grad.astype(jnp.bfloat16)[None], "task", split_axis=4, concat_axis=0, tiled=True
    )
    trunk_gnorm = routed.astype(jnp.float32) * mask * silu_slope(trunk_norm)
    trunk_grad = norm_backward(trunk_gnorm, trunk_norm, trunk_inv, mask, valid_count).astype(
        jnp.bfloat16
    )
    trunk_kgrad = kernel_grads(full_in, trunk_grad, "ihwc,tihwo->tco", 1)
    input_part = input_grads(trunk_grad, jnp.swapaxes(trunk_full, 1, 2), "tihwo,oc->ihwc")
    input_grad = lax.psum_scatter(input_part, "task", scatter_dimension=3, tiled=True) * mask
    trunk_red, conv_red, second_red, first_red = (
        lax.psum_scatter(trunk_kgrad, "dp", scatter_dimension=2, tiled=True),
        lax.psum_scatter(conv_kgrad, "dp", scatter_dimension=1, tiled=True),
        lax.psum_scatter(second_kgrad, "dp", scatter_dimension=0, tiled=True),
        lax.psum_scatter(first_kgrad, "dp", scatter_dimension=0, tiled=True),
    )
    gram_raw = lax.psum(
        jnp.einsum("tkio,skio->ts", trunk_red, trunk_red, precision=highest), ("dp", "task")
    )
    channel_count = trunk_full.shape[1]
    all_pixels = images * lax.axis_size("dp") * height * across
    task_gram = gram_raw / jnp.float32(9 * channel_count * channel_count * all_pixels)
    combined = pcgrad_weights(gram_raw, conflicts)
    trunk_moment = moment_decay * trunk_momentum + jnp.einsum(
        "t,tkio->kio", combined, trunk_red, precision=highest
    )
    first_moment = moment_decay * first_momentum + first_red[None]
    second_moment = moment_decay * second_momentum + second_red[None]
    conv_moment = moment_decay * conv_momentum[0] + conv_red
    trunk_rows = lax.all_gather(trunk_moment, "task", axis=2, tiled=True)
    trunk_sq, first_sq, second_sq, conv_sq = lax.psum(
        (
            jnp.sum(trunk_rows * trunk_rows),
            jnp.sum(first_moment * first_moment),
            jnp.sum(second_moment * second_moment),
            jnp.sum(conv_moment * conv_moment),
        ),
        "dp",
    )
    trunk_ortho = trunk_rows / (jnp.sqrt(trunk_sq) + 1e-07)
    first_ortho = first_moment / (jnp.sqrt(first_sq) + 1e-07)
    second_ortho = second_moment / (jnp.sqrt(second_sq) + 1e-07)
    conv_ortho = conv_moment / (jnp.sqrt(conv_sq) + 1e-07)
    for sweep in range(NS_STEPS):
        trunk_gram, first_gram, second_gram, conv_gram = lax.psum(
            (
                gram_local(trunk_ortho),
                gram_local(first_ortho),
                gram_local(second_ortho),
                gram_local(conv_ortho),
            ),
            "dp",
        )
        trunk_ortho = ns_update(trunk_ortho, trunk_gram)
        first_ortho = ns_update(first_ortho, first_gram)
        second_ortho = ns_update(second_ortho, second_gram)
        conv_ortho = ns_update(conv_ortho, conv_gram)
    block_width = trunk_weight.shape[2]
    trunk_block = lax.dynamic_slice_in_dim(
        trunk_ortho, lax.axis_index("task") * block_width, block_width, 2
    )
    shrink = 1.0 - step_rate * weight_decay
    trunk_new = shrink * trunk_weight - step_rate * trunk_block
    first_new = shrink * attn_first - step_rate * first_ortho
    second_new = shrink * attn_second - step_rate * second_ortho
    conv_new = shrink * branch_conv - step_rate * conv_ortho[None]
    return (
        features,
        input_grad,
        trunk_new,
        first_new,
        second_new,
        conv_new,
        trunk_moment,
        first_moment,
        second_moment,
        conv_moment[None],
        task_gram,
    )


def solution(mesh):
    placed = (
        P("dp", None, None, "task"),
        P("dp", None),
        P(),
        P(None, "dp", "task"),
        P("task", "dp", None),
        P("task", "dp", None),
        P("task", None, "dp", None),
        P(None, "dp", "task"),
        P("task", "dp", None),
        P("task", "dp", None),
        P("task", None, "dp", None),
        P("task", "dp", None, None, None),
    )
    return jax.shard_map(
        body,
        mesh=mesh,
        in_specs=placed,
        out_specs=(
            P("task", "dp", None, None, None),
            P("dp", None, None, "task"),
            P(None, "dp", "task"),
            P("task", "dp", None),
            P("task", "dp", None),
            P("task", None, "dp", None),
            P(None, "dp", "task"),
            P("task", "dp", None),
            P("task", "dp", None),
            P("task", None, "dp", None),
            P(),
        ),
        check_vma=False,
    )
```

profile of v0, /device:TPU:0, one launch (start us, length us, event | category | flops | bytes accessed | tf_op | source)
XLA Modules:
  0.0 1724.9 jit_solution(4561723112416976688)
XLA Ops:
  15.6 39.0 %all-gather.12.cloned.1.call-done = bf16[9,512,128]{2,1,0:T(8,128)(2,1)} async-done(((bf16[9,64,128]{2,1,0:T(8,128)(2,1)}), bf16[9,512,128]{2,1,0:T(8,128)(2,1)}) %all-gather.12.cloned.1.call-update) | async-done | bytes 1179664 | tf_op jit(solution)/shard_map/all_gather | solution.py:143
  54.6 20.8 %all-gather.10.cloned.1.call-done = bf16[1,32,48,512]{3,2,1,0:T(8,128)(2,1)} async-done(((bf16[1,32,48,128]{3,2,1,0:T(8,128)(2,1)}), bf16[1,32,48,512]{3,2,1,0:T(8,128)(2,1)}) %all-gather.10.cloned.1.call-update) | async-done | bytes 1572880 | tf_op jit(solution)/shard_map/all_gather | solution.py:141
  83.3 22.0 %all-reduce.13 = (f32[128]{0:T(128)S(1)}, f32[]{:T(128)}, f32[128]{0:T(128)S(1)}) all-reduce(f32[128]{0:T(128)S(1)} %get-tuple-element.35, f32[]{:T(128)} %convert_reduce_fusion.9, f32[128]{0:T(128)S(1)} %get-tuple-element.34), channel_id=1, replica_groups=mesh['dp'=8,'task'=4] {'dp'}, use_global_device_ids=true, to_apply=%region_1.2 | all-reduce | flops 257 | bytes 2056 | tf_op jit(solution)/shard_map/psum | solution.py:57
  116.6 34.5 %all-gather.1 = bf16[1,512,512]{2,1,0:T(8,128)(2,1)} all-gather(bf16[1,64,512]{2,1,0:T(8,128)(2,1)S(1)} %convert_element_type.360), channel_id=3, replica_groups=mesh['dp'=8,'task'=4] {'dp'}, dimensions={1}, use_global_device_ids=true | all-gather | bytes 589824 | tf_op jit(solution)/shard_map/all_gather | solution.py:144
  151.1 34.8 %all-gather.2 = bf16[1,512,512]{2,1,0:T(8,128)(2,1)} all-gather(bf16[1,64,512]{2,1,0:T(8,128)(2,1)S(1)} %convert_element_type.363), channel_id=4, replica_groups=mesh['dp'=8,'task'=4] {'dp'}, dimensions={1}, use_global_device_ids=true | all-gather | bytes 589824 | tf_op jit(solution)/shard_map/all_gather | solution.py:145
  188.5 17.7 %all-reduce.12 = (f32[512]{0:T(512)S(1)}, f32[512]{0:T(512)S(1)}) all-reduce(f32[512]{0:T(512)S(1)} %get-tuple-element.31, f32[512]{0:T(512)S(1)} %get-tuple-element.30), channel_id=1, replica_groups=mesh['dp'=8,'task'=4] {'dp'}, use_global_device_ids=true, to_apply=%region_9.10 | all-reduce | flops 1024 | bytes 8192 | tf_op jit(solution)/shard_map/psum | solution.py:57
  210.7 18.9 %all-reduce.11 = (f32[512]{0:T(512)S(1)}, f32[512]{0:T(512)S(1)}) all-reduce(f32[512]{0:T(512)S(1)} %get-tuple-element.29, f32[512]{0:T(512)S(1)} %get-tuple-element.28), channel_id=1, replica_groups=mesh['dp'=8,'task'=4] {'dp'}, use_global_device_ids=true, to_apply=%region_13.14 | all-reduce | flops 1024 | bytes 8192 | tf_op jit(solution)/shard_map/psum | solution.py:57
  256.4 17.3 %all-reduce.10 = (f32[512]{0:T(512)S(1)}, f32[512]{0:T(512)S(1)}) all-reduce(f32[512]{0:T(512)S(1)} %get-tuple-element.27, f32[512]{0:T(512)S(1)} %get-tuple-element.26), channel_id=1, replica_groups=mesh['dp'=8,'task'=4] {'dp'}, use_global_device_ids=true, to_apply=%region_17.18 | all-reduce | flops 1024 | bytes 8192 | tf_op jit(solution)/shard_map/psum | solution.py:57
  278.0 19.4 %all-reduce.9 = (f32[512]{0:T(512)S(1)}, f32[512]{0:T(512)S(1)}) all-reduce(f32[512]{0:T(512)S(1)} %get-tuple-element.14, f32[512]{0:T(512)S(1)} %get-tuple-element.13), channel_id=1, replica_groups=mesh['dp'=8,'task'=4] {'dp'}, use_global_device_ids=true, to_apply=%region_22.23 | all-reduce | flops 1024 | bytes 8192 | tf_op jit(solution)/shard_map/psum | solution.py:74
  325.6 9.3 fusion.366
  335.0 17.3 %all-reduce.8 = (f32[512]{0:T(512)S(1)}, f32[512]{0:T(512)S(1)}) all-reduce(f32[512]{0:T(512)S(1)} %get-tuple-element.12, f32[512]{0:T(512)S(1)} %get-tuple-element.11), channel_id=1, replica_groups=mesh['dp'=8,'task'=4] {'dp'}, use_global_device_ids=true, to_apply=%region_26.27 | all-reduce | flops 1024 | bytes 8192 | tf_op jit(solution)/shard_map/psum | solution.py:74
  361.2 19.1 %all-reduce.7 = (f32[512]{0:T(512)S(1)}, f32[512]{0:T(512)S(1)}) all-reduce(f32[512]{0:T(512)S(1)} %get-tuple-element.33, f32[512]{0:T(512)S(1)} %get-tuple-element.32), channel_id=1, replica_groups=mesh['dp'=8,'task'=4] {'dp'}, use_global_device_ids=true, to_apply=%region_30.31 | all-reduce | flops 1024 | bytes 8192 | tf_op jit(solution)/shard_map/psum | solution.py:74
  442.4 17.5 %all-reduce.6 = (f32[4,128]{1,0:T(4,128)S(1)}, f32[4,128]{1,0:T(4,128)S(1)}) all-reduce(f32[4,128]{1,0:T(4,128)S(1)} %get-tuple-element.16, f32[4,128]{1,0:T(4,128)S(1)} %get-tuple-element.15), channel_id=1, replica_groups=mesh['dp'=8,'task'=4] {'dp'}, use_global_device_ids=true, to_apply=%region_34.35 | all-reduce | flops 1024 | bytes 8192 | tf_op jit(solution)/shard_map/psum | solution.py:74
  494.3 11.9 copy.174
  529.3 272.9 %all-reduce.22.cloned.1.call-done = f32[4,9,512,128]{3,0,1,2:T(4,128)} async-done(((f32[4,9,512,128]{3,0,1,2:T(4,128)}), f32[4,9,512,128]{3,0,1,2:T(4,128)}) %all-reduce.22.cloned.1.call-update) | async-done | bytes 9437200
  812.0 39.4 %psum.255 = f32[4,4]{1,0:T(4,128)S(1)} all-reduce(f32[4,4]{1,0:T(4,128)S(1)} %convolution_bitcast_fusion.21), channel_id=1, replica_groups=mesh['dp'=8,'task'=4] {'dp','task'}, use_global_device_ids=true, to_apply=%region_46.47 | all-reduce | flops 16 | bytes 128 | tf_op jit(solution)/shard_map/psum | solution.py:211
  884.9 49.9 %reduce-scatter.9.cloned.1.call-done = f32[64,512]{1,0:T(8,128)} async-done(((f32[512,512]{1,0:T(8,128)}), f32[64,512]{1,0:T(8,128)}) %reduce-scatter.9.cloned.1.call-update) | async-done | bytes 131088 | tf_op jit(solution)/shard_map/reduce_scatter | solution.py:208
  936.4 17.2 all-gather.14.cloned.1.call-done
  955.8 165.2 %reduce-scatter.11.cloned.1.call-done = f32[9,64,512]{2,1,0:T(8,128)} async-done(((f32[9,512,512]{2,1,0:T(8,128)}), f32[9,64,512]{2,1,0:T(8,128)}) %reduce-scatter.11.cloned.1.call-update) | async-done | bytes 1179664 | tf_op jit(solution)/shard_map/reduce_scatter | solution.py:207
  1124.1 20.1 %all-reduce.5 = (f32[]{:T(128)}, f32[]{:T(128)}, f32[]{:T(128)}, f32[]{:T(128)}) all-reduce(f32[]{:T(128)} %multiply_reduce_fusion.9, f32[]{:T(128)} %get-tuple-element.89, f32[]{:T(128)} %get-tuple-element.87, f32[]{:T(128)} %get-tuple-element.85), channel_id=1, replica_groups=mesh['dp'=8,'task'=4] {'dp'}, use_global_device_ids=true, to_apply=%region_60.61 | all-reduce | flops 4 | bytes 32 | tf_op jit(solution)/shard_map/psum | solution.py:225
  1168.3 144.9 %all-reduce.28.cloned.1.call-done = (f32[512,512]{1,0:T(8,128)}, f32[512,512]{1,0:T(8,128)}, f32[512,512]{1,0:T(8,128)}, f32[512,512]{1,0:T(8,128)}) async-done(((f32[512,512]{1,0:T(8,128)}, f32[512,512]{1,0:T(8,128)}, f32[512,512]{1,0:T(8,128)}, f32[512,512]{1,0:T(8,128)}), (f32[512,512]{1,0:T(8,128)}, f32[512,512]{1,0:T(8,128)}, f32[512,512]{1,0:T(8,128)}, ...) | async-done | bytes 4194320 | tf_op jit(solution)/shard_map/psum | solution.py:239
  1341.5 27.3 %convert_reduce_fusion.8 = (bf16[32,48,128]{1,0,2:T(8,128)(2,1)}, bf16[32,48,128]{1,0,2:T(8,128)(2,1)}, bf16[32,48,128]{1,0,2:T(8,128)(2,1)S(1)}, bf16[32,48,128...) fusion(bf16[4,1,32,48,128]{3,2,4,0,1:T(8,128)(2,1)} %fusion.7), kind=kLoop, calls=%fused_computation.25 | loop fusion | flops 12386304 | bytes 5111808 | tf_op jit(solution)/shard_map/tihwo,oc->ihwc/reduce_sum | solution.py:40
  1382.9 114.9 %all-reduce.26.cloned.1.call-done = (f32[512,512]{1,0:T(8,128)}, f32[512,512]{1,0:T(8,128)}, f32[512,512]{1,0:T(8,128)}, f32[512,512]{1,0:T(8,128)}) async-done(((f32[512,512]{1,0:T(8,128)}, f32[512,512]{1,0:T(8,128)}, f32[512,512]{1,0:T(8,128)}, f32[512,512]{1,0:T(8,128)}), (f32[512,512]{1,0:T(8,128)}, f32[512,512]{1,0:T(8,128)}, f32[512,512]{1,0:T(8,128)}, ...) | async-done | bytes 4194320 | tf_op jit(solution)/shard_map/psum | solution.py:239
  1539.9 159.2 %all-reduce.24.cloned.1.call-done = (f32[512,512]{1,0:T(8,128)}, f32[512,512]{1,0:T(8,128)}, f32[512,512]{1,0:T(8,128)}, f32[512,512]{1,0:T(8,128)}) async-done(((f32[512,512]{1,0:T(8,128)}, f32[512,512]{1,0:T(8,128)}, f32[512,512]{1,0:T(8,128)}, f32[512,512]{1,0:T(8,128)}), (f32[512,512]{1,0:T(8,128)}, f32[512,512]{1,0:T(8,128)}, f32[512,512]{1,0:T(8,128)}, ...) | async-done | bytes 4194320 | tf_op jit(solution)/shard_map/psum | solution.py:239
  (339 shorter events, 372.0 us)
Async XLA Ops:
  7.2 47.4 %all-gather.12.cloned.1.call-start = ((), (), s32[]{:S(2)}) async-start(), calls=%async_computation.6 | async-start | bytes 1327104 | tf_op jit(solution)/shard_map/all_gather | solution.py:143
  8.9 66.4 %all-gather.10.cloned.1.call-start = ((), (), s32[]{:S(2)}) async-start(), calls=%async_computation.5 | async-start | bytes 1966080 | tf_op jit(solution)/shard_map/all_gather | solution.py:141
  13.6 172.2 %all-gather.16.cloned.1.call-start = ((), (), s32[]{:S(2)}) async-start(), calls=%async_computation.12 | async-start | bytes 1966080 | tf_op jit(solution)/shard_map/all_gather | solution.py:151
  105.9 354.0 %copy-start.72 = (f32[128]{0:T(128)}, f32[128]{0:T(128)S(1)}, u32[]{:S(2)}) copy-start(f32[128]{0:T(128)S(1)} %get-tuple-element.97) | copy-start | bytes 1540
  109.4 123.8 %all-gather.18.cloned.1.call-start = ((), (), s32[]{:S(2)}) async-start(), calls=%async_computation.13 | async-start | bytes 5308416 | tf_op jit(solution)/shard_map/all_gather | solution.py:146
  404.2 24.5 %all-to-all-start = ((bf16[4,2,98304]{2,1,0:T(2,128)(2,1)}), bf16[4,2,98304]{2,1,0:T(2,128)(2,1)}, u32[]{:S(2)}, u32[]{:S(2)}) async-start(bf16[4,2,98304]{2,1,0:T(2,128)(2,1)} %reshape.837), calls=%async_computation | async-start | bytes 3145728 | tf_op jit(solution)/shard_map/all_to_all | solution.py:195
  408.6 393.7 %all-reduce.22.cloned.1.call-start = ((), (), s32[]{:S(2)}) async-start(), calls=%async_computation.14 | async-start | bytes 18874368
  506.3 376.3 %reduce-scatter.7.cloned.1.call-start = ((), (), s32[]{:S(2)}) async-start(), calls=%async_computation.9 | async-start | bytes 1179648 | tf_op jit(solution)/shard_map/reduce_scatter | solution.py:209
  520.8 414.1 %reduce-scatter.9.cloned.1.call-start = ((), (), s32[]{:S(2)}) async-start(), calls=%async_computation.10 | async-start | bytes 1179648 | tf_op jit(solution)/shard_map/reduce_scatter | solution.py:208
  529.2 424.3 %all-gather.14.cloned.1.call-start = ((), (), s32[]{:S(2)}) async-start(), calls=%async_computation.8 | async-start | bytes 1474560 | tf_op jit(solution)/shard_map/all_gather | solution.py:224
  810.0 63.4 %copy-start.62 = (f32[9,64,128]{2,1,0:T(8,128)S(1)}, f32[9,64,128]{2,1,0:T(8,128)}, u32[]{:S(2)}) copy-start(f32[9,64,128]{2,1,0:T(8,128)} %param.19) | copy-start | bytes 884740
  851.4 25.0 %copy-start.65 = (f32[4,4]{1,0:T(4,128)}, f32[4,4]{1,0:T(4,128)S(1)}, u32[]{:S(2)}) copy-start(f32[4,4]{1,0:T(4,128)S(1)} %psum.255) | copy-start | bytes 196
  874.2 246.8 %reduce-scatter.11.cloned.1.call-start = ((), (), s32[]{:S(2)}) async-start(), calls=%async_computation.11 | async-start | bytes 10616832 | tf_op jit(solution)/shard_map/reduce_scatter | solution.py:207
  882.4 52.4 %copy-start.64 = (f32[1,64,512]{2,1,0:T(8,128)S(1)}, f32[1,64,512]{2,1,0:T(8,128)}, u32[]{:S(2)}) copy-start(f32[1,64,512]{2,1,0:T(8,128)} %param.21) | copy-start | bytes 393220
  882.5 238.5 %copy-start.51 = (f32[1,9,64,512]{3,2,1,0:T(8,128)S(1)}, f32[1,9,64,512]{3,2,1,0:T(8,128)}, u32[]{:S(2)}) copy-start(f32[1,9,64,512]{3,2,1,0:T(8,128)} %param.22) | copy-start | bytes 3538948
  882.5 430.7 %all-reduce.28.cloned.1.call-start = ((), (), s32[]{:S(2)}) async-start(), calls=%async_computation.17 | async-start | bytes 8388608 | tf_op jit(solution)/shard_map/psum | solution.py:239
  884.9 440.2 %copy-start.42 = (f32[1,64,512]{2,1,0:T(8,128)}, f32[1,64,512]{2,1,0:T(8,128)S(1)}, u32[]{:S(2)}) copy-start(f32[1,64,512]{2,1,0:T(8,128)S(1)} %get-tuple-element.90) | copy-start | bytes 393220
  936.4 393.3 %copy-start.43 = (f32[1,64,512]{2,1,0:T(8,128)}, f32[1,64,512]{2,1,0:T(8,128)S(1)}, u32[]{:S(2)}) copy-start(f32[1,64,512]{2,1,0:T(8,128)S(1)} %get-tuple-element.88) | copy-start | bytes 393220
  1124.1 26.9 %copy-start.52 = (f32[9,64,512]{2,1,0:T(8,128)S(1)}, f32[9,64,512]{2,1,0:T(8,128)}, u32[]{:S(2)}) copy-start(f32[9,64,512]{2,1,0:T(8,128)} %get-tuple-element.86) | copy-start | bytes 3538948
  1158.4 339.4 %all-reduce.26.cloned.1.call-start = ((), (), s32[]{:S(2)}) async-start(), calls=%async_computation.16 | async-start | bytes 8388608 | tf_op jit(solution)/shard_map/psum | solution.py:239
  1168.3 149.1 %copy-start.45 = (f32[9,64,512]{2,1,0:T(8,128)S(1)}, f32[9,64,512]{2,1,0:T(8,128)}, u32[]{:S(2)}) copy-start(f32[9,64,512]{2,1,0:T(8,128)} %all-gather.14.cloned.1.call-done) | copy-start | bytes 3538948
  1341.4 195.6 %reduce-scatter.5.cloned.1.call-start = ((), (), s32[]{:S(2)}) async-start(), calls=%async_computation.7 | async-start | bytes 3932160 | tf_op jit(solution)/shard_map/reduce_scatter | solution.py:204
  1382.5 316.6 %all-reduce.24.cloned.1.call-start = ((), (), s32[]{:S(2)}) async-start(), calls=%async_computation.15 | async-start | bytes 8388608 | tf_op jit(solution)/shard_map/psum | solution.py:239
  1535.5 167.6 %copy-start.22 = (f32[9,64,512]{2,1,0:T(8,128)S(1)}, f32[9,64,512]{2,1,0:T(8,128)}, u32[]{:S(2)}) copy-start(f32[9,64,512]{2,1,0:T(8,128)} %copy-done.21) | copy-start | bytes 3538948
  (67 other events, 258.1 us)
Sparse Core Ops, SparseCore 0:
  10.8 43.7 all-gather.11
  56.7 18.5 all-gather.9
  109.5 16.1 all-gather.15
  127.7 86.2 all-gather.17
  506.4 295.7 all-reduce.21
  806.0 62.4 reduce-scatter.6
  872.3 62.4 reduce-scatter.8
  937.0 16.5 all-gather.13
  957.2 163.6 reduce-scatter.10
  1158.5 154.5 all-reduce.27
  1341.6 156.2 all-reduce.25
  1500.2 36.7 reduce-scatter.4
  1541.6 157.3 all-reduce.23
where the time goes:
time: 1730 us; the launch traced here: 1720 us
  waiting for transfers between devices  994 us (57%)
  blocking collectives  278 us (16%)
  matrix products  220 us (13%)
  other arithmetic  109 us (6%)
  local copies, waits for them, and re-layouts  75.8 us (4%)
  between operations  42.3 us (2%)
    psum x3, waiting for transfers between devices, body(): lax.psum((gram_local(trunk_ortho), gram_local(first_ortho), gram_local(se...  419 us
    unnamed x14, waiting for transfers between devices  273 us
    reduce_scatter x1, waiting for transfers between devices, body(): lax.psum_scatter(conv_kgrad, 'dp', scatter_dimension=1, tiled=True)  165 us
    psum x4, blocking collectives, norm_forward(): lax.psum((jnp.sum(values * mask, axis=(0, 1, 2)), jnp.sum(values * values...  75.9 us
    psum x4, blocking collectives, norm_backward(): lax.psum((jnp.sum(grad_norm, axis=(-4, -3, -2), keepdims=True), jnp.sum(g...  73.3 us
    reduce_scatter x1, waiting for transfers between devices, body(): lax.psum_scatter(second_kgrad, 'dp', scatter_dimension=0, tiled=True)  49.9 us
    dot_general x18, matrix products, input_grads(): jnp.einsum(spec, window, kernel[offset], preferred_element_type=jnp.float32)  43 us
    psum x1, blocking collectives, body(): lax.psum(jnp.einsum('tkio,skio->ts', trunk_red, trunk_red, precision=high...  39.4 us
  transfers between devices with their start and end apart: 14, of which 11 were waited for; matrix products, arithmetic and copies ran while one was open for 10% of the time, Pallas kernels for 0%

commit v1 on v0

v1 whole, which is shorter than its diff:
```python
import functools

import jax
import jax.numpy as jnp
from jax import lax
from jax.experimental import pallas as pl
from jax.experimental.pallas import tpu as pltpu
from jax.sharding import PartitionSpec as P

NS_STEPS = 3

epsilon = 1e-05
moment_decay = 0.95
step_rate = 1.0
weight_decay = 0.01
shrink = 1.0 - step_rate * weight_decay
coeff_a = 3.4445
coeff_b = -4.775
coeff_c = 2.0315
bf16 = jnp.bfloat16
f32 = jnp.float32
i32 = jnp.int32

LANES = 128
TAPS = 9
STEPS = 4


ABS, REL, RING_ABS, RING_REL, ME = 0, 8, 16, 24, 32

RING = (0, 2, 4, 6, 7, 5, 3, 1)
OFFSETS = (0, -1, -2, -3, -4, 1, 2, 3)


def by_chip():
    return lax.axis_size("dp") == 8 and lax.axis_size("task") == 4


def make_table():
    if not by_chip():
        return jnp.zeros((64,), i32)
    me = lax.axis_index("task")
    index = lax.axis_index("dp")
    pos = (jnp.where(index % 2 == 0, index // 2, 7 - index // 2) + jnp.array(OFFSETS, i32) + 8) % 8
    places = jnp.stack([index ^ jnp.arange(8, dtype=i32), jnp.where(pos < 4, 2 * pos, 15 - 2 * pos)])
    mixed = ((places // 2) ^ me) * 2 + places % 2
    return jnp.concatenate([places[0], mixed[0], places[1], mixed[1], jnp.full((32,), me, i32)])


def ring_gather(shard):
    if not by_chip():
        return [lax.all_gather(shard, "dp", axis=shard.ndim - 2, tiled=True)]
    ahead, behind = [shard], [shard]
    for step in range(4):
        ahead.append(lax.ppermute(ahead[-1], "dp", [(RING[p], RING[(p + 1) % 8]) for p in range(8)]))
        if step < 3:
            behind.append(lax.ppermute(behind[-1], "dp", [(RING[p], RING[p - 1]) for p in range(8)]))
    return ahead + behind[1:]


def flip_dp(value, mask):
    return lax.ppermute(value, "dp", [(i, i ^ mask) for i in range(8)])


def gather_dp(shard):
    if not by_chip():
        return [lax.all_gather(shard, "dp", axis=shard.ndim - 2, tiled=True)]
    far = flip_dp(shard, 4)
    near = [flip_dp(shard, k) for k in (1, 2, 3)]
    return [shard] + near + [far] + [flip_dp(far, k) for k in (1, 2, 3)]


def scatter_dp(terms, deps=()):
    if not by_chip():
        (whole,) = terms
        copies = lax.axis_size("dp")
        whole = whole.reshape((copies, whole.shape[0] // copies) + whole.shape[1:]).astype(f32)
        return [lax.psum_scatter(whole, "dp", scatter_dimension=0, tiled=False)]
    got = [flip_dp(terms[4 + k], k) for k in (1, 2, 3)]
    near = terms[1:4]
    if deps:
        shape, dtype = terms[4].shape, terms[4].dtype
        beyond, *near = call(
            beyond_kernel,
            "beyond",
            [(v, WHOLE) for v in [terms[4]] + got] + [(v, REMAIN) for v in near],
            [(shape, dtype, WHOLE)] + [(shape, dtype, REMAIN)] * 3,
            us=1,
            deps=deps,
            aliases={4: 1, 5: 2, 6: 3},
        )
    else:
        beyond = (terms[4].astype(f32) + got[0].astype(f32)) + (got[1].astype(f32) + got[2].astype(f32))
    far = flip_dp(beyond.astype(terms[4].dtype), 4)
    return [terms[0]] + [flip_dp(v, k + 1) for k, v in enumerate(near)] + [far]


def beyond_kernel(term, g1, g2, g3, n1, n2, n3, out, o1, o2, o3):
    value = (term[...].astype(f32) + g1[...].astype(f32)) + (g2[...].astype(f32) + g3[...].astype(f32))
    out[...] = value.astype(out.dtype)


def wide_scatter(whole):
    copies = lax.axis_size("dp")
    whole = whole.reshape((copies, whole.shape[0] // copies) + whole.shape[1:])
    if not by_chip():
        whole = whole.astype(f32)
    return [lax.psum_scatter(whole, "dp", scatter_dimension=0, tiled=False)]


def exchange(values):
    if not by_chip():
        return lax.psum(values, "dp")
    near = [flip_dp(values, k) for k in (1, 2, 3)]
    half = (values + near[0]) + (near[1] + near[2])
    return half + flip_dp(half, 4)


def flip_task(value, mask):
    return lax.ppermute(value, "task", [(i, i ^ mask) for i in range(4)])


def gather_task(block):
    if not by_chip():
        whole = lax.all_gather(block, "task", axis=0, tiled=False)
        return [whole[t] for t in range(4)]
    core = flip_task(block, 1)
    chip = flip_task(block, 2)
    return [block, core, chip, flip_task(chip, 1)]


def route_task(blocks):
    if not by_chip():
        got = lax.all_to_all(jnp.stack(blocks), "task", 0, 0)
        return [got[t] for t in range(4)]
    return [blocks[0], flip_task(blocks[1], 1), flip_task(blocks[2], 2), flip_task(blocks[3], 3)]


def add_task(blocks):
    if not by_chip():
        return lax.psum_scatter(jnp.stack(blocks).astype(f32), "task", scatter_dimension=0, tiled=False)
    beyond = blocks[2].astype(f32) + flip_task(blocks[3], 1).astype(f32)
    near = blocks[0].astype(f32) + flip_task(blocks[1], 1).astype(f32)
    return near + flip_task(beyond.astype(bf16), 2).astype(f32)


WHOLE = pl.BlockSpec(memory_space=pltpu.VMEM)
SCALARS = pl.BlockSpec(memory_space=pltpu.SMEM)
REMAIN = pl.BlockSpec(memory_space=pl.ANY)


def room(shape, dtype, spec):
    if spec is SCALARS or spec is REMAIN:
        return 0
    dims = shape if spec is WHOLE else spec.block_shape
    size = jnp.dtype(dtype).itemsize
    dims = (1,) * (2 - len(dims)) + tuple(dims)
    lead = 1
    for d in dims[:-2]:
        lead *= d
    bytes_ = lead * -(-dims[-2] // 16) * 16 * -(-dims[-1] // LANES) * LANES * size
    return bytes_ if spec is WHOLE or spec.pipeline_mode is not None else 2 * bytes_


def call(kernel, name, ins, outs, scratch=(), grid=(), us=4.0, deps=(), aliases=None, spare=5):
    moved = sum(a.size * a.dtype.itemsize for a, _ in ins)
    shapes = [jax.ShapeDtypeStruct(s, d) for s, d, _ in outs]
    moved += sum(s.size * s.dtype.itemsize for s in shapes)
    need = spare * 1024 * 1024
    need += sum(room(a.shape, a.dtype, spec) for a, spec in ins) + sum(room(*out) for out in outs)
    need += sum(room(v.shape, v.dtype, WHOLE) for v in scratch if getattr(v, "memory_space", None) == pltpu.VMEM)
    skip = len(deps)
    return pl.pallas_call(
        lambda *refs: kernel(*refs[skip:]),
        name=name,
        grid=grid,
        in_specs=[REMAIN] * skip + [s for _, s in ins],
        out_specs=[s for _, _, s in outs],
        out_shape=shapes,
        scratch_shapes=list(scratch),
        input_output_aliases={skip + k: v for k, v in (aliases or {}).items()},
        compiler_params=pltpu.CompilerParams(vmem_limit_bytes=min(need, 58 * 1024 * 1024)),
        cost_estimate=pl.CostEstimate(flops=int(us * 0.3e9), bytes_accessed=int(moved), transcendentals=0),
    )(*deps, *[a for a, _ in ins])


def fixed(array):
    rank = array.ndim
    return (array, pl.BlockSpec(array.shape, lambda i: (0,) * rank, pipeline_mode=pl.Buffered(1)))


def now(array, rows):
    return (array, pl.BlockSpec((rows, array.shape[1]), lambda i: (jnp.minimum(i, STEPS - 1), 0)))


def before(array, rows):
    return (array, pl.BlockSpec((rows, array.shape[1]), lambda i: (jnp.maximum(i - 1, 0), 0)))


def out_now(rows, cols, count, dtype):
    return ((rows * count, cols), dtype, pl.BlockSpec((rows, cols), lambda i: (jnp.minimum(i, count - 1), 0)))


def out_before(rows, cols, count, dtype):
    return ((rows * count, cols), dtype, pl.BlockSpec((rows, cols), lambda i: (jnp.maximum(i - 1, 0), 0)))


def out_fixed(shape, dtype):
    return (shape, dtype, pl.BlockSpec(shape, lambda i: (0,) * len(shape)))


def wide(value, columns):
    return jnp.concatenate([value] * (columns // LANES), axis=1)


def fold(value):
    rows, columns = value.shape
    return jnp.sum(value.reshape(rows // 8, 8, columns), axis=0)


def edges(rows, across, columns):
    place = lax.broadcasted_iota(i32, (across, LANES), 0)
    first = jnp.where(place == 0, 0.0, 1.0)
    last = jnp.where(place == across - 1, 0.0, 1.0)
    return tuple(wide(jnp.concatenate([e] * (rows // across), axis=0), columns) for e in (first, last))


def step_back(value, first):
    return pltpu.roll(value, 1, axis=0) * first


def step_on(value, last):
    return pltpu.roll(value, value.shape[0] - 1, axis=0) * last


def sigmoid(value):
    return 0.5 * jnp.tanh(0.5 * value) + 0.5


def slope(value):
    sigma = sigmoid(value)
    return sigma * (1.0 + value * (1.0 - sigma))


def dot(a, b):
    return jnp.dot(a, b, preferred_element_type=f32)


def dot_last(a, b):
    return lax.dot_general(a, b, (((1,), (1,)), ((), ())), preferred_element_type=f32)


def dot_first(a, b):
    return lax.dot_general(a, b, (((0,), (0,)), ((), ())), preferred_element_type=f32)


def norm_terms(stats, trunk):
    total = jnp.sum(stats[...], axis=0)
    valid = wide(trunk[2:3, :], total.shape[1])
    mean = total[0:1] / valid
    return mean, lax.rsqrt(total[1:2] / valid - mean * mean + epsilon)


def back_terms(stats, trunk):
    total = jnp.sum(stats[...], axis=0)
    valid = wide(trunk[2:3, :], total.shape[1])
    return total[0:1] / valid, total[1:2] / valid


def put_rows(ref, acc):
    for k in range(ref.shape[1]):
        row = jnp.sum(acc[8 * k : 8 * k + 8, :], axis=0, keepdims=True)
        for j in range(ref.shape[0]):
            ref[j, k : k + 1, :] = row


def put_chunks(outs, table, first, whole):
    for k, out in enumerate(outs):
        size = out.shape[0]
        out[...] = whole[pl.ds(pl.multiple_of(table[first + k] * size, size), size), :].astype(out.dtype)


def place_chunks(chunks, table, first, dest, sems):
    copies = []
    for k, chunk in enumerate(chunks):
        rows = chunk.shape[-2]
        at = pl.ds(pl.multiple_of(table[first + k] * rows, rows), rows)
        slot = dest.at[at, :] if len(chunk.shape) == 2 else dest.at[:, at, :]
        copies.append(pltpu.make_async_copy(chunk, slot, sems.at[k]))
    return copies


def mask_kernel(rows, across, extents, mask):
    i = pl.program_id(0)
    place = lax.broadcasted_iota(i32, (across, LANES), 0)
    for line in range(rows // across):
        reach = jnp.where(i * (rows // across) + line < extents[0, 0], extents[0, 1], 0)
        mask[pl.ds(line * across, across), :] = jnp.where(place < reach, 1.0, 0.0)


def low_kernel(values, out):
    out[...] = values[...].astype(bf16)


def pair_low_kernel(first, second, out):
    columns = first.shape[1]
    out[:, 0:columns] = first[...].astype(bf16)
    out[:, columns:] = second[...].astype(bf16)


def turn_kernel(count, *rest):
    blocks, out = rest[:count], rest[-1]
    values = [b[...] for b in blocks]
    if len(rest) > count + 1:
        keep = rest[count][...].astype(bf16)
        values = [v * keep for v in values]
    out[...] = jnp.concatenate(values, axis=1).T


def trunk_kernel(rows, across, count, table, x0, x1, x2, x3, hide, mask, *rest):
    chunks = rest[:count]
    out, stats, weights, terms, acc, sems = rest[count:]
    i = pl.program_id(0)
    depth = terms.shape[1] // TAPS

    @pl.when(i == 0)
    def _():
        copies = place_chunks(chunks, table, RING_REL, weights, sems)
        for c in copies:
            c.start()
        terms[0:across, :] = jnp.zeros((across, terms.shape[1]), f32)
        terms[pl.ds(terms.shape[0] - across, across), :] = jnp.zeros((across, terms.shape[1]), f32)
        acc[...] = jnp.zeros_like(acc)
        for c in copies:
            c.wait()

    @pl.when(i < STEPS)
    def _():
        keep = hide[...].astype(bf16)
        values = jnp.concatenate([x[...] * keep for x in (x0, x1, x2, x3)], axis=1)
        terms[pl.ds(pl.multiple_of(across + i * rows, across), rows), :] = dot(values, weights[...])

    @pl.when(i > 0)
    def _():
        base = (i - 1) * rows
        first, last = edges(rows, across, depth)
        sides = []
        for b in range(3):
            side = None
            for a in range(3):
                at = pl.ds(pl.multiple_of(base + a * across, across), rows)
                term = terms[at, (3 * a + b) * depth : (3 * a + b + 1) * depth]
                side = term if side is None else side + term
            sides.append(side)
        value = sides[1] + step_back(sides[0], first) + step_on(sides[2], last)
        out[...] = value
        keep = mask[...]
        kept = value * keep
        acc[0:8, :] += fold(kept)
        acc[8:16, :] += fold(kept * value)
        acc[16:24, :] += fold(keep)

    @pl.when(i == STEPS)
    def _():
        put_rows(stats, acc)


def shared_kernel(pre, stats, mask, part, trunk):
    total = jnp.sum(stats[...], axis=0)
    valid = total[2:3]
    mean = total[0:1] / valid
    inverse = lax.rsqrt(total[1:2] / valid - mean * mean + epsilon)
    trunk[0:1, :] = mean
    trunk[1:2, :] = inverse
    trunk[2:3, :] = valid
    trunk[3:8, :] = jnp.zeros((5, LANES), f32)
    normed = (pre[...] - mean) * inverse
    part[...] = (mask[...] * normed * sigmoid(normed)).astype(bf16)


def first_kernel(count, table, x0, x1, x2, x3, mask, *rest):
    chunks = rest[:count]
    pre, shared, stats, kept_weights, weights, acc, sems = rest[count:]
    i = pl.program_id(0)

    @pl.when(i == 0)
    def _():
        copies = place_chunks(chunks, table, RING_ABS, kept_weights, sems)
        for c in copies:
            c.start()
        acc[...] = jnp.zeros_like(acc)
        for c in copies:
            c.wait()
        for r in range(4):
            at = pl.ds(pl.multiple_of((table[ME] ^ r) * LANES, LANES), LANES)
            weights[r * LANES : (r + 1) * LANES, :] = kept_weights[at, 0 : pre.shape[1]]

    blocks = [x0[...], x1[...], x2[...], x3[...]]
    me = table[ME]
    for r, block in enumerate(blocks):
        shared[:, pl.ds(pl.multiple_of((me ^ r) * LANES, LANES), LANES)] = block
    value = dot(jnp.concatenate(blocks, axis=1), weights[...])
    pre[...] = value
    kept = value * wide(mask[...], value.shape[1])
    acc[0:8, :] += fold(kept)
    acc[8:16, :] += fold(kept * value)

    @pl.when(i == STEPS - 1)
    def _():
        put_rows(stats, acc)


def second_kernel(pre, mask, stats1, trunk, weights, out, hidden, stats, acc):
    i = pl.program_id(0)

    @pl.when(i == 0)
    def _():
        acc[...] = jnp.zeros_like(acc)

    mean, inverse = norm_terms(stats1, trunk)
    keep = wide(mask[...], pre.shape[1])
    normed = (pre[...] - mean) * inverse
    low = (keep * normed * sigmoid(normed)).astype(bf16)
    hidden[...] = low
    value = dot(low, weights[:, out.shape[1] :])
    out[...] = value
    kept = value * keep
    acc[0:8, :] += fold(kept)
    acc[8:16, :] += fold(kept * value)

    @pl.when(i == STEPS - 1)
    def _():
        put_rows(stats, acc)


def clear_ends(padded, across):
    zero = jnp.zeros((across, padded.shape[1]), padded.dtype)
    padded[0:across, :] = zero
    padded[pl.ds(padded.shape[0] - across, across), :] = zero


def branch_kernel(rows, across, count, table, pre, shared, stats2, trunk, mask, *rest):
    chunks = rest[:count]
    out, merged, stats, weights, sides, acc, sems = rest[count:]
    i = pl.program_id(0)
    depth = pre.shape[1]
    copies = place_chunks(chunks, table, ABS, weights, sems)

    @pl.when(i == 0)
    def _():
        for c in copies:
            c.start()
        clear_ends(sides, across)
        acc[...] = jnp.zeros_like(acc)

    @pl.when(i < STEPS)
    def _():
        mean, inverse = norm_terms(stats2, trunk)
        gate = sigmoid((pre[...] - mean) * inverse)
        low = (gate * shared[...].astype(f32)).astype(bf16)
        merged[...] = low
        first, last = edges(rows, across, depth)
        value = low.astype(f32)
        at = pl.ds(pl.multiple_of(across + i * rows, across), rows)
        sides[at, 0:depth] = step_back(value, first).astype(bf16)
        sides[at, depth : 2 * depth] = low
        sides[at, 2 * depth : 3 * depth] = step_on(value, last).astype(bf16)

    @pl.when(i == 1)
    def _():
        for c in copies:
            c.wait()

    @pl.when(i > 0)
    def _():
        base = (i - 1) * rows
        value = None
        for a in range(3):
            at = pl.ds(pl.multiple_of(base + a * across, across), rows)
            term = dot(sides[at, :], weights[3 * a : 3 * a + 3].reshape(3 * depth, depth))
            value = term if value is None else value + term
        out[...] = value
        kept = value * wide(mask[...], depth)
        acc[0:8, :] += fold(kept)
        acc[8:16, :] += fold(kept * value)

    @pl.when(i == STEPS)
    def _():
        put_rows(stats, acc)


def pool_kernel(pre, cot, spread, mask, stats4, trunk, features, grad, stats, acc):
    i = pl.program_id(0)

    @pl.when(i == 0)
    def _():
        acc[...] = jnp.zeros_like(acc)

    mean, inverse = norm_terms(stats4, trunk)
    keep = wide(mask[...], pre.shape[1])
    normed = (pre[...] - mean) * inverse
    sigma = sigmoid(normed)
    active = keep * normed * sigma
    high = active.astype(bf16)
    low = (active - high.astype(f32)).astype(bf16)
    ups = spread[...]
    pooled = dot_first(ups, high) + dot_first(ups, low)
    features[...] = (0.25 * pooled).astype(bf16)
    value = dot(ups, cot[...]) * 0.25 * keep * (sigma * (1.0 + normed * (1.0 - sigma)))
    grad[...] = value
    acc[0:8, :] += fold(value)
    acc[8:16, :] += fold(value * normed)

    @pl.when(i == STEPS - 1)
    def _():
        put_rows(stats, acc)


def branch_back_kernel(
    rows, across, count, table, pre, grad, mask, stats4, back4, trunk, pre2, shared, stats2, *rest
):
    chunks = rest[:count]
    delta, gate_grad, shared_grad, stats, weights, sides, acc, sems = rest[count:]
    i = pl.program_id(0)
    depth = pre.shape[1]
    copies = place_chunks(chunks, table, ABS, weights, sems)

    @pl.when(i == 0)
    def _():
        for c in copies:
            c.start()
        clear_ends(sides, across)
        acc[...] = jnp.zeros_like(acc)

    @pl.when(i < STEPS)
    def _():
        mean, inverse = norm_terms(stats4, trunk)
        one, two = back_terms(back4, trunk)
        keep = wide(mask[...], depth)
        normed = (pre[...] - mean) * inverse
        low = (inverse * (grad[...] - keep * (one + normed * two))).astype(bf16)
        delta[...] = low
        first, last = edges(rows, across, depth)
        value = low.astype(f32)
        at = pl.ds(pl.multiple_of(across + i * rows, across), rows)
        sides[at, 0:depth] = step_on(value, last).astype(bf16)
        sides[at, depth : 2 * depth] = low
        sides[at, 2 * depth : 3 * depth] = step_back(value, first).astype(bf16)

    @pl.when(i == 1)
    def _():
        for c in copies:
            c.wait()

    @pl.when(i > 0)
    def _():
        base = (i - 1) * rows
        value = None
        for a in range(3):
            at = pl.ds(pl.multiple_of(base + (2 - a) * across, across), rows)
            for b in range(3):
                term = dot_last(sides[at, b * depth : (b + 1) * depth], weights[3 * a + b])
                value = term if value is None else value + term
        mean, inverse = norm_terms(stats2, trunk)
        normed = (pre2[...] - mean) * inverse
        gate = sigmoid(normed)
        shared_grad[...] = value * gate
        inner = value * shared[...].astype(f32) * (gate * (1.0 - gate))
        gate_grad[...] = inner
        acc[0:8, :] += fold(inner)
        acc[8:16, :] += fold(inner * normed)

    @pl.when(i == STEPS)
    def _():
        put_rows(stats, acc)


def branch_weight_kernel(rows, across, count, table, delta, turned, *rest):
    outs = rest[:count]
    sides, whole = rest[count:]
    i = pl.program_id(0)
    depth = delta.shape[1]
    pixels = turned.shape[1]

    @pl.when(i == 0)
    def _():
        clear_ends(sides, across)

    @pl.when(i < STEPS)
    def _():
        first, last = edges(rows, across, depth)
        low = delta[...]
        value = low.astype(f32)
        at = pl.ds(pl.multiple_of(across + i * rows, across), rows)
        sides[at, 0:depth] = step_on(value, last).astype(bf16)
        sides[at, depth : 2 * depth] = low
        sides[at, 2 * depth : 3 * depth] = step_back(value, first).astype(bf16)

    @pl.when(i >= STEPS)
    def _():
        at = pl.ds(pl.multiple_of((2 - (i - STEPS)) * across, across), pixels)
        whole[...] = dot(turned[...], sides[at, :])
        put_chunks(outs, table, ABS, whole)


def second_back_kernel(
    gate_grad, pre2, pre1, mask, back2, stats2, stats1, trunk, weights, delta, grad, stats, acc
):
    i = pl.program_id(0)
    depth = pre1.shape[1]

    @pl.when(i == 0)
    def _():
        acc[...] = jnp.zeros_like(acc)

    keep = wide(mask[...], depth)
    mean, inverse = norm_terms(stats2, trunk)
    one, two = back_terms(back2, trunk)
    normed = (pre2[...] - mean) * inverse
    low = (inverse * (gate_grad[...] - keep * (one + normed * two))).astype(bf16)
    delta[...] = low
    mean, inverse = norm_terms(stats1, trunk)
    normed = (pre1[...] - mean) * inverse
    value = dot_last(low, weights[:, depth:]) * keep * slope(normed)
    grad[...] = value
    acc[0:8, :] += fold(value)
    acc[8:16, :] += fold(value * normed)

    @pl.when(i == STEPS - 1)
    def _():
        put_rows(stats, acc)


def first_back_kernel(
    table, grad, pre1, mask, back1, stats1, trunk, shared_grad, weights, delta, b0, b1, b2, b3, whole
):
    depth = pre1.shape[1]

    keep = wide(mask[...], depth)
    mean, inverse = norm_terms(stats1, trunk)
    one, two = back_terms(back1, trunk)
    normed = (pre1[...] - mean) * inverse
    low = (inverse * (grad[...] - keep * (one + normed * two))).astype(bf16)
    delta[...] = low
    whole[...] = (shared_grad[...] + dot_last(low, weights[:, 0:depth])).astype(bf16)
    me = table[ME]
    for r, block in enumerate((b0, b1, b2, b3)):
        block[...] = whole[:, pl.ds(pl.multiple_of((me ^ r) * LANES, LANES), LANES)]


def pair_weight_kernel(count, table, shared, delta1, hidden, delta2, *rest):
    outs = rest[:count]
    (whole,) = rest[count:]
    depth = shared.shape[1]
    whole[:, 0:depth] = dot_first(shared[...], delta1[...])
    whole[:, depth:] = dot_first(hidden[...], delta2[...])
    put_chunks(outs, table, ABS, whole)


def trunk_sums_kernel(g0, g1, g2, g3, pre, mask, trunk, stats, acc):
    i = pl.program_id(0)

    @pl.when(i == 0)
    def _():
        acc[...] = jnp.zeros_like(acc)

    normed = (pre[...] - trunk[0:1, :]) * trunk[1:2, :]
    scale = mask[...] * slope(normed)
    for r, g in enumerate((g0, g1, g2, g3)):
        value = g[...].astype(f32) * scale
        acc[16 * r : 16 * r + 8, :] += fold(value)
        acc[16 * r + 8 : 16 * r + 16, :] += fold(value * normed)

    @pl.when(i == STEPS - 1)
    def _():
        put_rows(stats, acc)


def trunk_weight_kernel(
    rows, across, count, table, g0, g1, g2, g3, pre, mask, trunk, back, turned, *rest
):
    outs = rest[:count]
    delta, sides, whole = rest[count:]
    i = pl.program_id(0)
    depth = 4 * LANES
    pixels = turned.shape[1]

    @pl.when(i == 0)
    def _():
        clear_ends(sides, across)

    @pl.when(i < STEPS)
    def _():
        mean, inverse, valid = trunk[0:1, :], trunk[1:2, :], trunk[2:3, :]
        normed = (pre[...] - mean) * inverse
        keep = mask[...]
        scale = keep * slope(normed)
        total = jnp.sum(back[...], axis=0) / valid
        lows = []
        for r, g in enumerate((g0, g1, g2, g3)):
            value = g[...].astype(f32) * scale
            value = inverse * (value - keep * (total[2 * r : 2 * r + 1] + normed * total[2 * r + 1 : 2 * r + 2]))
            lows.append(value.astype(bf16))
        delta[...] = sum(low.astype(f32) for low in lows).astype(bf16)
        low = jnp.concatenate(lows, axis=1)
        first, last = edges(rows, across, depth)
        value = low.astype(f32)
        at = pl.ds(pl.multiple_of(across + i * rows, across), rows)
        sides[at, 0:depth] = step_on(value, last).astype(bf16)
        sides[at, depth : 2 * depth] = low
        sides[at, 2 * depth : 3 * depth] = step_back(value, first).astype(bf16)

    @pl.when(i >= STEPS)
    def _():
        at = pl.ds(pl.multiple_of((2 - (i - STEPS)) * across, across), pixels)
        whole[...] = dot(turned[...], sides[at, :])
        put_chunks(outs, table, REL, whole)


def input_kernel(rows, across, delta, weights, b0, b1, b2, b3, sides):
    i = pl.program_id(0)
    depth = delta.shape[1]

    @pl.when(i == 0)
    def _():
        clear_ends(sides, across)

    @pl.when(i < STEPS)
    def _():
        first, last = edges(rows, across, depth)
        low = delta[...]
        value = low.astype(f32)
        at = pl.ds(pl.multiple_of(across + i * rows, across), rows)
        sides[at, 0:depth] = step_on(value, last).astype(bf16)
        sides[at, depth : 2 * depth] = low
        sides[at, 2 * depth : 3 * depth] = step_back(value, first).astype(bf16)

    @pl.when(i > 0)
    def _():
        base = (i - 1) * rows
        value = None
        for a in range(3):
            at = pl.ds(pl.multiple_of(base + (2 - a) * across, across), rows)
            term = dot_last(sides[at, :], weights[:, 3 * a * depth : 3 * (a + 1) * depth])
            value = term if value is None else value + term
        for r, block in enumerate((b0, b1, b2, b3)):
            block[...] = value[:, r * LANES : (r + 1) * LANES].astype(bf16)


def trunk_total_kernel(count, copies, table, *rest):
    terms = rest[:count]
    total, grams = rest[count:]
    value = sum(t[...].astype(f32) for t in terms)
    total[...] = value
    me = table[ME]
    for r in range(4):
        for s in range(r, 4):
            part = None
            for tap in range(TAPS):
                left = value[:, (4 * tap + r) * LANES : (4 * tap + r + 1) * LANES]
                right = value[:, (4 * tap + s) * LANES : (4 * tap + s + 1) * LANES]
                part = left * right if part is None else part + left * right
            entry = jnp.sum(fold(part), axis=0, keepdims=True)
            entry = jnp.broadcast_to(jnp.sum(entry, axis=1, keepdims=True), (1, LANES))
            for j in range(copies):
                grams[j, pl.ds((me ^ r) * 4 + (me ^ s), 1), :] = entry
                if r != s:
                    grams[j, pl.ds((me ^ s) * 4 + (me ^ r), 1), :] = entry


def trunk_moment_kernel(table, flags, gram, total, momentum, moment, low, rest):
    entry = [[gram[4 * t + s : 4 * t + s + 1, :] for s in range(4)] for t in range(4)]
    combined = [jnp.zeros((1, LANES), f32) for _ in range(4)]
    for target in range(4):
        coeffs = [jnp.full((1, LANES), 1.0 if t == target else 0.0, f32) for t in range(4)]
        for source in range(4):
            if source != target:
                inner = sum(coeffs[t] * entry[t][source] for t in range(4))
                flag = flags[target, source].astype(f32)
                coeffs[source] = coeffs[source] - flag * inner / entry[source][source]
        combined = [combined[t] + coeffs[t] for t in range(4)]
    me = table[ME]
    mixed = []
    for r in range(4):
        mixed.append(sum(jnp.where((me ^ r) == t, combined[t], 0.0) for t in range(4)))
    values = []
    for tap in range(TAPS):
        value = moment_decay * momentum[tap]
        for r in range(4):
            value = value + mixed[r] * total[:, (4 * tap + r) * LANES : (4 * tap + r + 1) * LANES]
        moment[tap] = value
        values.append(value)
    low[...], rest[...] = split(jnp.concatenate(values, axis=0))


def trunk_gram_kernel(table, m0, m1, m2, m3, whole, parts):
    me = table[ME]
    for r, m in enumerate((m0, m1, m2, m3)):
        whole[:, pl.ds(pl.multiple_of((me ^ r) * LANES, LANES), LANES)] = m[...]
    value = dot_first(m0[...], whole[...])
    size = parts.shape[1]
    for d in range(parts.shape[0]):
        parts[d] = value[d * size : (d + 1) * size]


def spread_kernel(parts, out):
    value = jnp.sum(parts[...], axis=0)
    for d in range(out.shape[0]):
        out[d] = value


def split(value):
    high = value.astype(bf16)
    return high, (value - high.astype(f32)).astype(bf16)


def dot_split(a, b):
    return dot(a[0], b[0]) + (dot(a[0], b[1]) + dot(a[1], b[0]))


def dot_even(a, b):
    left = jnp.concatenate([a[0], a[0], a[1]], axis=1)
    right = jnp.concatenate([b[0], b[1], b[0]], axis=0)
    half = left.shape[0] // 2
    top = dot(left[:half], right)
    corner = dot(left[half:], right[:, half:])
    return jnp.concatenate([top, jnp.concatenate([top[:, half:].T, corner], axis=1)], axis=0)


def newton_schulz(gram, place=None):
    size = gram.shape[0]
    same = lax.broadcasted_iota(i32, (size, size), 0) == lax.broadcasted_iota(i32, (size, size), 1)
    diagonal = jnp.sum(fold(jnp.where(same, gram, 0.0)), axis=0, keepdims=True)
    norm = jnp.sqrt(jnp.sum(diagonal, axis=1, keepdims=True)) + 1e-07
    scale = 1.0 / norm
    value = gram * (scale * scale)
    product = None
    for sweep in range(NS_STEPS):
        parts = split(value)
        step = coeff_b * value + coeff_c * dot_even(parts, parts) + jnp.where(same, coeff_a, 0.0)
        if sweep < NS_STEPS - 1:
            pair = split(step)
            value = dot_even(split(dot_even(pair, parts)), pair)
            product = pair if sweep == 0 else split(dot_even(product, pair))
    if place is not None:
        return dot_split(product, split(place(step))) * scale
    return dot_even(product, split(step)) * scale


def trunk_new_kernel(table, g0, g1, g2, g3, r0, r1, r2, r3, whole, weight, out, gram, last, rest):
    me = table[ME]
    for r, g in enumerate((g0, g1, g2, g3)):
        gram[pl.ds(pl.multiple_of((me ^ r) * LANES, LANES), LANES), :] = g[...]
    for r, m in enumerate((r0, r1, r2, r3)):
        rest[:, pl.ds(pl.multiple_of((me ^ r) * LANES, LANES), LANES)] = m[...]
    own = pl.ds(pl.multiple_of(table[ME + 1] * LANES, LANES), LANES)

    def place(step):
        last[...] = step
        return last[:, own]

    turn = newton_schulz(gram[...], place)
    value = dot_split((whole[...], rest[...]), split(turn))
    depth = weight.shape[1]
    for tap in range(TAPS):
        out[tap] = shrink * weight[tap] - step_rate * value[tap * depth : (tap + 1) * depth]


def conv_moment_kernel(count, table, *rest):
    terms = rest[:count]
    momentum, moment, *parts, gram = rest[count:]
    columns = momentum.shape[2]
    lows = []
    for tap in range(TAPS):
        at = slice(tap * columns, (tap + 1) * columns)
        value = moment_decay * momentum[tap] + sum(t[:, at].astype(f32) for t in terms)
        moment[tap] = value
        lows.append(value)
    low = jnp.concatenate(lows, axis=0).astype(bf16)
    gram[...] = dot_first(low, low)
    put_chunks(parts, table, ABS, gram)


def conv_new_kernel(count, table, *rest):
    chunks = rest[:count]
    moment, weight, out, gram, sems = rest[count:]
    copies = place_chunks(chunks, table, ABS, gram, sems)
    for c in copies:
        c.start()
    for c in copies:
        c.wait()
    turn = newton_schulz(gram[...])
    value = dot_split(split(moment[...]), split(turn))
    depth = weight.shape[1]
    for tap in range(TAPS):
        out[tap] = shrink * weight[tap] - step_rate * value[tap * depth : (tap + 1) * depth]


def pair_moment_kernel(count, *rest):
    terms = rest[:count]
    momentum1, momentum2, moment1, moment2, low = rest[count:]
    columns = momentum1.shape[1]
    value = sum(t[...].astype(f32) for t in terms)
    one = moment_decay * momentum1[...] + value[:, 0:columns]
    two = moment_decay * momentum2[...] + value[:, columns:]
    moment1[...] = one
    moment2[...] = two
    low[:, 0:columns] = one.astype(bf16)
    low[:, columns:] = two.astype(bf16)


def pair_new_kernel(*refs):
    chunks, (moment1, moment2, weight1, weight2, out1, out2) = refs[:-6], refs[-6:]
    columns = weight1.shape[1]
    every = jnp.concatenate([c[...] for c in chunks], axis=0)
    for k, (moment, weight, out) in enumerate(((moment1, weight1, out1), (moment2, weight2, out2))):
        half = every[:, k * columns : (k + 1) * columns]
        turn = newton_schulz(dot_first(half, half))
        out[...] = shrink * weight[...] - step_rate * dot_split(split(moment[...]), split(turn))


def body(
    inputs,
    extents,
    conflicts,
    trunk_weight,
    attn_first,
    attn_second,
    branch_conv,
    trunk_momentum,
    first_momentum,
    second_momentum,
    conv_momentum,
    cotangent,
):
    height, across = (inputs.shape[1], inputs.shape[2])
    pixels = height * across
    rows = pixels // STEPS
    depth, width = trunk_weight.shape[1], trunk_weight.shape[2]
    channels = attn_first.shape[2]
    devices = lax.axis_size("dp")
    n = 1
    table = make_table()
    scal = (table, SCALARS)
    slots = 8 if by_chip() else 1

    def dma(count):
        return pltpu.SemaphoreType.DMA((count,))

    def remain(chunks):
        return [(c, REMAIN) for c in chunks]

    def vmem(*shape, dtype=f32):
        return pltpu.VMEM(shape, dtype)

    full_in = gather_task(inputs.reshape(pixels, width))
    trunk_chunks = ring_gather(jnp.swapaxes(trunk_weight.astype(bf16), 0, 1).reshape(depth, TAPS * width))
    (pair_low,) = call(
        pair_low_kernel,
        "pair_low",
        [(attn_first[0], WHOLE), (attn_second[0], WHOLE)],
        [((depth, 2 * channels), bf16, WHOLE)],
        us=1,
    )
    pair_chunks = ring_gather(pair_low)
    (conv_low,) = call(
        low_kernel,
        "low",
        [(branch_conv[0], WHOLE)],
        [((TAPS, depth, channels), bf16, WHOLE)],
        us=1.5,
    )
    conv_chunks = [lax.all_gather(conv_low, "dp", axis=1, tiled=True)]
    whole_table = (jnp.zeros((8,), i32), SCALARS)
    count = len(trunk_chunks)
    (mask,) = call(
        functools.partial(mask_kernel, rows, across),
        "mask",
        [(extents, SCALARS)],
        [out_now(rows, width, STEPS, f32)],
        grid=(STEPS,),
        us=2,
    )
    trunk_pre, sums, trunk_weights = call(
        functools.partial(trunk_kernel, rows, across, count),
        "trunk",
        [scal] + [now(x, rows) for x in full_in] + [now(mask, rows), before(mask, rows)] + remain(trunk_chunks),
        [
            out_before(rows, width, STEPS, f32),
            out_fixed((n, 3, width), f32),
            out_fixed((channels, TAPS * width), bf16),
        ],
        [
            vmem(pixels + 2 * across, TAPS * width),
            vmem(24, width),
            dma(count),
        ],
        (STEPS + 1,),
        us=7,
        deps=[pair_chunks[2], pair_chunks[6]] if by_chip() else [],
    )
    sums = exchange(sums)
    shared_part, trunk = call(
        shared_kernel,
        "shared",
        [now(trunk_pre, rows), fixed(sums), now(mask, rows)],
        [out_now(rows, width, STEPS, bf16), out_fixed((8, width), f32)],
        grid=(STEPS,),
        us=3,
        deps=[pair_chunks[3], pair_chunks[7]] if by_chip() else [],
    )
    shared_blocks = gather_task(shared_part)

    first_pre, shared, sums, weights = call(
        functools.partial(first_kernel, count),
        "first",
        [scal] + [now(x, rows) for x in shared_blocks] + [now(mask, rows)] + remain(pair_chunks),
        [
            out_now(rows, channels, STEPS, f32),
            out_now(rows, channels, STEPS, bf16),
            out_fixed((n, 2, channels), f32),
            out_fixed((channels, 2 * channels), bf16),
        ],
        [vmem(channels, channels, dtype=bf16), vmem(16, channels), dma(count)],
        (STEPS,),
        us=6,
    )
    stats1 = exchange(sums)
    second_pre, hidden, sums = call(
        second_kernel,
        "second",
        [now(first_pre, rows), now(mask, rows), fixed(stats1), fixed(trunk), fixed(weights)],
        [
            out_now(rows, channels, STEPS, f32),
            out_now(rows, channels, STEPS, bf16),
            out_fixed((n, 2, channels), f32),
        ],
        [vmem(16, channels)],
        (STEPS,),
        us=6,
        spare=36,
    )
    stats2 = exchange(sums)
    sides = vmem(pixels + 2 * across, 3 * channels, dtype=bf16)
    conv_pre, merged, sums = call(
        functools.partial(branch_kernel, rows, across, 1),
        "branch",
        [
            whole_table,
            now(second_pre, rows),
            now(shared, rows),
            fixed(stats2),
            fixed(trunk),
            before(mask, rows),
        ]
        + remain(conv_chunks),
        [
            out_before(rows, channels, STEPS, f32),
            out_now(rows, channels, STEPS, bf16),
            out_fixed((n, 2, channels), f32),
        ],
        [vmem(TAPS, channels, channels, dtype=bf16), sides, vmem(16, channels), dma(1)],
        (STEPS + 1,),
        us=13,
        spare=30,
    )
    stats4 = exchange(sums)

    def turn(blocks, hide, name):
        return call(
            functools.partial(turn_kernel, len(blocks)),
            name,
            [now(v, rows) for v in blocks] + [now(v, rows) for v in hide],
            [((channels, pixels), bf16, pl.BlockSpec((channels, rows), lambda i: (0, i)))],
            grid=(STEPS,),
            us=3,
        )[0]

    pool_rows = rows // 4
    line = jnp.arange(rows) // across
    spot = (line // 2) * (across // 2) + (jnp.arange(rows) % across) // 2
    spread = (spot[:, None] == jnp.arange(pool_rows)[None, :]).astype(bf16)
    features, grad, sums = call(
        pool_kernel,
        "pool",
        [
            now(conv_pre, rows),
            now(cotangent.reshape(pixels // 4, channels), pool_rows),
            fixed(spread),
            now(mask, rows),
            fixed(stats4),
            fixed(trunk),
        ],
        [
            out_now(pool_rows, channels, STEPS, bf16),
            out_now(rows, channels, STEPS, f32),
            out_fixed((n, 2, channels), f32),
        ],
        [vmem(16, channels)],
        (STEPS,),
        us=6,
    )
    back4 = exchange(sums)
    conv_delta, gate_grad, shared_grad, sums = call(
        functools.partial(branch_back_kernel, rows, across, 1),
        "branch_back",
        [
            whole_table,
            now(conv_pre, rows),
            now(grad, rows),
            now(mask, rows),
            fixed(stats4),
            fixed(back4),
            fixed(trunk),
            before(second_pre, rows),
            before(shared, rows),
            fixed(stats2),
        ]
        + remain(conv_chunks),
        [
            out_now(rows, channels, STEPS, bf16),
            out_before(rows, channels, STEPS, f32),
            out_before(rows, channels, STEPS, f32),
            out_fixed((n, 2, channels), f32),
        ],
        [vmem(TAPS, channels, channels, dtype=bf16), sides, vmem(16, channels), dma(1)],
        (STEPS + 1,),
        us=15,
    )
    back2 = exchange(sums)
    merged_turned = turn([merged], [], "merged_turn")
    (conv_term,) = call(
        functools.partial(branch_weight_kernel, rows, across, 1),
        "branch_weight",
        [whole_table, now(conv_delta, rows), fixed(merged_turned)],
        [
            (
                (channels, TAPS * channels),
                bf16,
                pl.BlockSpec((channels, 3 * channels), lambda i: (0, jnp.maximum(i - STEPS, 0))),
            )
        ],
        [sides, vmem(channels, 3 * channels)],
        (STEPS + 3,),
        us=10,
    )
    conv_parts = wide_scatter(conv_term)
    second_delta, first_grad, sums = call(
        second_back_kernel,
        "second_back",
        [
            now(gate_grad, rows),
            now(second_pre, rows),
            now(first_pre, rows),
            now(mask, rows),
            fixed(back2),
            fixed(stats2),
            fixed(stats1),
            fixed(trunk),
            fixed(weights),
        ],
        [
            out_now(rows, channels, STEPS, bf16),
            out_now(rows, channels, STEPS, f32),
            out_fixed((n, 2, channels), f32),
        ],
        [vmem(16, channels)],
        (STEPS,),
        us=5,
        spare=36,
        deps=[conv_term],
    )
    back1 = exchange(sums)
    first_delta, *blocks = call(
        first_back_kernel,
        "first_back",
        [
            scal,
            now(first_grad, rows),
            now(first_pre, rows),
            now(mask, rows),
            fixed(back1),
            fixed(stats1),
            fixed(trunk),
            now(shared_grad, rows),
            fixed(weights),
        ],
        [out_now(rows, channels, STEPS, bf16)] + [out_now(rows, width, STEPS, bf16)] * 4,
        [vmem(rows, channels, dtype=bf16)],
        (STEPS,),
        us=4,
    )
    routed = route_task(blocks)
    pair_terms = call(
        functools.partial(pair_weight_kernel, slots),
        "pair_weight",
        [scal] + [(v, WHOLE) for v in (shared, first_delta, hidden, second_delta)],
        [((channels // slots, 2 * channels), bf16, WHOLE)] * slots,
        [vmem(channels, 2 * channels)],
        us=3,
        deps=routed[1:2],
    )

    pair_parts = scatter_dp(pair_terms)
    first_moment, second_moment, pair_low = call(
        functools.partial(pair_moment_kernel, len(pair_parts)),
        "pair_moment",
        [(v, WHOLE) for v in pair_parts] + [(first_momentum[0], WHOLE), (second_momentum[0], WHOLE)],
        [
            ((depth, channels), f32, WHOLE),
            ((depth, channels), f32, WHOLE),
            ((depth, 2 * channels), bf16, WHOLE),
        ],
        us=2,
    )
    pair_moments = gather_dp(pair_low)

    (sums,) = call(
        trunk_sums_kernel,
        "trunk_sums",
        [now(g, rows) for g in routed] + [now(trunk_pre, rows), now(mask, rows), fixed(trunk)],
        [out_fixed((n, 8, width), f32)],
        [vmem(64, width)],
        (STEPS,),
        us=2,
    )
    back0 = exchange(sums)
    input_turned = turn(full_in, [mask], "input_turn")
    chunk = channels // slots
    *trunk_terms, delta_total = call(
        functools.partial(trunk_weight_kernel, rows, across, slots),
        "trunk_weight",
        [scal]
        + [now(g, rows) for g in routed]
        + [now(trunk_pre, rows), now(mask, rows), fixed(trunk), fixed(back0), fixed(input_turned)],
        [
            (
                (chunk, TAPS * 4 * width),
                bf16,
                pl.BlockSpec((chunk, 12 * width), lambda i: (0, jnp.maximum(i - STEPS, 0))),
            )
        ]
        * slots
        + [out_now(rows, width, STEPS, bf16)],
        [vmem(pixels + 2 * across, 12 * width, dtype=bf16), vmem(channels, 12 * width)],
        (STEPS + 3,),
        us=6,
        deps=pair_moments[1:],
    )
    input_blocks = call(
        functools.partial(input_kernel, rows, across),
        "input",
        [now(delta_total, rows), fixed(trunk_weights)],
        [out_before(rows, width, STEPS, bf16)] * 4,
        [vmem(pixels + 2 * across, 3 * width, dtype=bf16)],
        (STEPS + 1,),
        us=6,
    )
    conv_moment, *conv_grams = call(
        functools.partial(conv_moment_kernel, len(conv_parts)),
        "conv_moment",
        [scal] + [(v.reshape(depth, -1), WHOLE) for v in conv_parts] + [(conv_momentum[0], WHOLE)],
        [((TAPS, depth, channels), f32, WHOLE)] + [((channels // slots, channels), f32, WHOLE)] * slots,
        [vmem(channels, channels)],
        us=3,
        deps=trunk_terms[:1],
    )
    trunk_parts = scatter_dp(trunk_terms, deps=[input_blocks[0]])
    input_grad = (add_task(input_blocks) * mask).reshape(inputs.shape)

    if by_chip():
        conv_grams = scatter_dp(conv_grams)
        conv_gram = (conv_grams[0] + conv_grams[1]) + (conv_grams[2] + conv_grams[3]) + conv_grams[4]
        conv_grams = gather_dp(conv_gram)
    else:
        conv_gram = lax.psum(conv_grams[0], "dp")
        conv_grams = [conv_gram]
    first_new, second_new = call(
        pair_new_kernel,
        "pair_new",
        [(v, WHOLE) for v in pair_moments]
        + [(v, WHOLE) for v in (first_moment, second_moment, attn_first[0], attn_second[0])],
        [((depth, channels), f32, WHOLE)] * 2,
        us=18,
    )
    (conv_new,) = call(
        functools.partial(conv_new_kernel, len(conv_grams)),
        "conv_new",
        [scal]
        + remain(conv_grams)
        + [(v, WHOLE) for v in (conv_moment.reshape(TAPS * depth, channels), branch_conv[0])],
        [((TAPS, depth, channels), f32, WHOLE)],
        [vmem(channels, channels), dma(len(conv_grams))],
        us=11,
        spare=44,
    )

    everyone = 4 * devices if by_chip() else 1
    trunk_total, grams = call(
        functools.partial(trunk_total_kernel, len(trunk_parts), everyone),
        "trunk_total",
        [scal] + [(v, WHOLE) for v in trunk_parts],
        [((depth, TAPS * 4 * width), f32, WHOLE), ((everyone, 16, width), f32, WHOLE)],
        us=3,
        deps=[first_new] if by_chip() else [],
    )
    if by_chip():
        grams = lax.all_to_all(grams, ("dp", "task"), 0, 0)
        gram_rows = jnp.sum(grams, axis=0)
    else:
        gram_rows = lax.psum(grams[0], ("dp", "task"))
    all_pixels = inputs.shape[0] * devices * pixels
    task_gram = gram_rows[:, 0].reshape(4, 4) / jnp.float32(TAPS * channels * channels * all_pixels)
    trunk_moment, trunk_low, trunk_rest = call(
        trunk_moment_kernel,
        "trunk_moment",
        [scal, (conflicts, SCALARS), (gram_rows, WHOLE), (trunk_total, WHOLE), (trunk_momentum, WHOLE)],
        [((TAPS, depth, width), f32, WHOLE)] + [((TAPS * depth, width), bf16, WHOLE)] * 2,
        us=2.5,
        deps=[conv_gram] if by_chip() else [],
    )
    lows = gather_task(trunk_low)
    rests = gather_task(trunk_rest)
    if by_chip():
        trunk_whole, trunk_part = call(
            trunk_gram_kernel,
            "trunk_gram",
            [scal] + [(v, WHOLE) for v in lows],
            [
                ((TAPS * depth, channels), bf16, WHOLE),
                ((devices, width // devices, channels), f32, WHOLE),
            ],
            us=2,
        )
        trunk_part = lax.all_to_all(trunk_part, "dp", 0, 0)
        (gram_own,) = call(
            spread_kernel,
            "trunk_gram_own",
            [(trunk_part, WHOLE)],
            [((devices, width // devices, channels), f32, WHOLE)],
            us=1,
            deps=conv_grams[1:5] + rests[1:],
        )
        gram_blocks = gather_task(lax.all_to_all(gram_own, "dp", 0, 0).reshape(width, channels))
    else:
        trunk_whole = jnp.concatenate(lows, axis=1)
        trunk_part = jnp.einsum("ro,rp->op", trunk_low, trunk_whole, preferred_element_type=f32)
        gram_blocks = gather_task(lax.psum(trunk_part, "dp"))
    (trunk_new,) = call(
        trunk_new_kernel,
        "trunk_new",
        [(table.at[ME + 1].set(lax.axis_index("task")), SCALARS)]
        + [(v, WHOLE) for v in gram_blocks + rests + [trunk_whole, trunk_weight]],
        [((TAPS, depth, width), f32, WHOLE)],
        [vmem(channels, channels), vmem(channels, channels), vmem(TAPS * depth, channels, dtype=bf16)],
        us=11,
        deps=[conv_new] if by_chip() else [],
    )
    return (
        features.reshape(cotangent.shape),
        input_grad,
        trunk_new,
        first_new[None],
        second_new[None],
        conv_new[None],
        trunk_moment,
        first_moment[None],
        second_moment[None],
        conv_moment[None],
        task_gram,
    )


def solution(mesh):
    placed = (
        P("dp", None, None, "task"),
        P("dp", None),
        P(),
        P(None, "dp", "task"),
        P("task", "dp", None),
        P("task", "dp", None),
        P("task", None, "dp", None),
        P(None, "dp", "task"),
        P("task", "dp", None),
        P("task", "dp", None),
        P("task", None, "dp", None),
        P("task", "dp", None, None, None),
    )
    return jax.shard_map(
        body,
        mesh=mesh,
        in_specs=placed,
        out_specs=(
            P("task", "dp", None, None, None),
            P("dp", None, None, "task"),
            P(None, "dp", "task"),
            P("task", "dp", None),
            P("task", "dp", None),
            P("task", None, "dp", None),
            P(None, "dp", "task"),
            P("task", "dp", None),
            P("task", "dp", None),
            P("task", None, "dp", None),
            P(),
        ),
        check_vma=False,
    )
```

time: 1730 us -> 484 us (0.28)
  waiting for transfers between devices: 994 us -> 178 us
  blocking collectives: 278 us -> 0 us
  matrix products: 220 us -> 0 us
  starting transfers between devices: 5.88 us -> 133 us
  Pallas kernels: 0 us -> 126 us
  other arithmetic: 109 us -> 5.53 us
  local copies, waits for them, and re-layouts: 75.8 us -> 21.6 us
  between operations: 42.3 us -> 15.1 us
    psum x3 -> x0, waiting for transfers between devices: 419 us -> none  [body(): lax.psum((gram_local(trunk_ortho), gram_local(first_ortho), gram_local(se...]
    unnamed x14 -> x2, waiting for transfers between devices: 273 us -> 0.03 us
    dot_general x98 -> x0, matrix products: 220 us -> none  [the longest x18 43 us: input_grads(): jnp.einsum(spec, window, kernel[offset], preferred_element_type=jnp.float32)]
    reduce_scatter x4 -> x1, waiting for transfers between devices: 217 us -> 0.02 us  [wide_scatter(): return [lax.psum_scatter(whole, 'dp', scatter_dimension=0, tiled=False)]]
    psum x10 -> x0, blocking collectives: 209 us -> none  [the longest x4 75.9 us: norm_forward(): lax.psum((jnp.sum(values * mask, axis=(0, 1, 2)), jnp.sum(values * values...]
    ppermute x0 -> x102, waiting for transfers between devices: none -> 175 us  [the longest x67 131 us: flip_dp(): return lax.ppermute(value, 'dp', [(i, i ^ mask) for i in range(8)])]
    pallas_call x0 -> x29, Pallas kernels: none -> 126 us  [call(): pl.pallas_call(lambda *refs: kernel(*refs[skip:]), name=name, grid=grid,...]
    ppermute x0 -> x102, starting transfers between devices: none -> 122 us  [the longest x67 89.2 us: flip_dp(): return lax.ppermute(value, 'dp', [(i, i ^ mask) for i in range(8)])]
  transfers between devices with their start and end apart: 14 -> 107, of which waited for: 11 -> 62; matrix products, arithmetic and copies ran while one was open for 10% -> 1% of each run, Pallas kernels for 0% -> 16%
where the time goes in v1:
time: 484 us; the launch traced here: 480 us
  waiting for transfers between devices  178 us (37%)
  starting transfers between devices  133 us (27%)
  Pallas kernels  126 us (26%)
  local copies, waits for them, and re-layouts  21.6 us (4%)
  between operations  15.1 us (3%)
  other arithmetic  5.53 us (1%)
    ppermute x67, waiting for transfers between devices, flip_dp(): return lax.ppermute(value, 'dp', [(i, i ^ mask) for i in range(8)])  131 us
    pallas_call x29, Pallas kernels, call(): pl.pallas_call(lambda *refs: kernel(*refs[skip:]), name=name, grid=grid,...  126 us
    ppermute x67, starting transfers between devices, flip_dp(): return lax.ppermute(value, 'dp', [(i, i ^ mask) for i in range(8)])  89.2 us
    unnamed x128, local copies, waits for them, and re-layouts  20.9 us
    ppermute x21, waiting for transfers between devices, flip_task(): return lax.ppermute(value, 'task', [(i, i ^ mask) for i in range(4)])  17.3 us
    ppermute x8, starting transfers between devices, ring_gather(): lax.ppermute(ahead[-1], 'dp', [(RING[p], RING[(p + 1) % 8]) for p in rang...  16.9 us
    ppermute x6, waiting for transfers between devices, ring_gather(): lax.ppermute(behind[-1], 'dp', [(RING[p], RING[p - 1]) for p in range(8)])  15.2 us
    ppermute x8, waiting for transfers between devices, ring_gather(): lax.ppermute(ahead[-1], 'dp', [(RING[p], RING[(p + 1) % 8]) for p in rang...  11.3 us
  transfers between devices with their start and end apart: 107, of which 62 were waited for; matrix products, arithmetic and copies ran while one was open for 1% of the time, Pallas kernels for 16%

profile of v1, /device:TPU:0, one launch (start us, length us, event | category | flops | bytes accessed | tf_op | source)
XLA Modules:
  0.0 479.6 jit_solution(14089565947065577116)
XLA Ops:
  32.2 4.5 collective-permute-done.14.refs_15_
  36.6 4.8 %collective-permute-start.12 = (bf16[64,1152]{1,0:T(8,128)(2,1)S(1)}, bf16[64,1152]{1,0:T(8,128)(2,1)}, u32[]{:S(2)}, u32[]{:S(2)}) collective-permute-start(bf16[64,1152]{1,0:T(8,128)(2,1)S(1)} %collective-permute-done.11.refs_12_), channel_id=1, source_target_pairs={{0,8},{8,16},{16,24},{24,28},{28,20},{20,12},{12,4},{4,0},{1,9},{9... | collective-permute-start | bytes 442376 | tf_op jit(solution)/shard_map/ppermute | solution.py:55
  45.4 6.7 %collective-permute-done.15.refs_16_ = bf16[64,1152]{1,0:T(8,128)(2,1)S(1)} collective-permute-done((bf16[64,1152]{1,0:T(8,128)(2,1)S(1)}, bf16[64,1152]{1,0:T(8,128)(2,1)S(1)}, u32[]{:S(2)}, u32[]{:S(2)}) %collective-permute-start.15) | collective-permute-done | bytes 147488 | tf_op jit(solution)/shard_map/ppermute | solution.py:57
  52.2 5.8 %trunk.1 = (f32[1536,128]{1,0:T(8,128)S(1)}, f32[1,3,128]{2,1,0:T(4,128)S(1)}, bf16[512,1152]{1,0:T(8,128)(2,1)S(1)}) custom-call(bf16[64,1024]{1,0:T(8,128)(2,1)S(1)} %copy-done.47, bf16[64,1024]{1,0:T(8,128)(2,1)} %collective-permute-done.4.refs_1_.refs_12_, s32[64]{0:T(128)S(1)} %concatenate.5.refs_2_.refs_0_.refs_1_.refs_7_, ...), custom_call_target="tpu_custom_call" | custom-call | flops 2100000000 | bytes 6293248 | tf_op jit(solution)/shard_map/trunk/pallas_call | solution.py:173
  66.2 7.3 %collective-permute-done.19 = f32[1,3,128]{2,1,0:T(4,128)S(1)} collective-permute-done((f32[1,3,128]{2,1,0:T(4,128)S(1)}, f32[1,3,128]{2,1,0:T(4,128)S(1)}, u32[]{:S(2)}, u32[]{:S(2)}) %collective-permute-start.19) | collective-permute-done | bytes 1568 | tf_op jit(solution)/shard_map/ppermute | solution.py:62
  75.5 6.5 %collective-permute-done.21.refs_3_ = bf16[1536,128]{1,0:T(8,128)(2,1)S(1)} collective-permute-done((bf16[1536,128]{1,0:T(8,128)(2,1)S(1)}, bf16[1536,128]{1,0:T(8,128)(2,1)S(1)}, u32[]{:S(2)}, u32[]{:S(2)}) %collective-permute-start.21) | collective-permute-done | bytes 393248 | tf_op jit(solution)/shard_map/ppermute | solution.py:120
  82.6 7.4 %collective-permute-done.23.refs_10_ = bf16[64,1024]{1,0:T(8,128)(2,1)S(1)} collective-permute-done((bf16[64,1024]{1,0:T(8,128)(2,1)S(1)}, bf16[64,1024]{1,0:T(8,128)(2,1)S(1)}, u32[]{:S(2)}, u32[]{:S(2)}) %collective-permute-start.23) | collective-permute-done | bytes 131104 | tf_op jit(solution)/shard_map/ppermute | solution.py:55
  95.0 6.5 %collective-permute-start.26 = (f32[1,2,512]{2,1,0:T(2,128)S(1)}, f32[1,2,512]{2,1,0:T(2,128)S(1)}, u32[]{:S(2)}, u32[]{:S(2)}) collective-permute-start(f32[1,2,512]{2,1,0:T(2,128)S(1)} %get-tuple-element.103), channel_id=1, source_target_pairs={{0,12},{4,8},{8,4},{12,0},{16,28},{20,24},{24,20},{28,16},{1,13},{... | collective-permute-start | bytes 12296 | tf_op jit(solution)/shard_map/ppermute | solution.py:62
  124.3 12.6 %branch.1 = (f32[1536,512]{1,0:T(8,128)S(1)}, bf16[1536,512]{1,0:T(8,128)(2,1)S(1)}, f32[1,2,512]{2,1,0:T(2,128)S(1)}) custom-call(s32[8]{0:T(128)S(1)} %broadcast_18_refs_0_.2.refs_0_, f32[1536,512]{1,0:T(8,128)} %copy-done.3, bf16[1536,512]{1,0:T(8,128)(2,1)S(1)} %get-tuple-element.107.refs_2_.refs_8_, f32[1,2,512]{2,1,0:T(2,128)S(1)} %add.219.refs_3_.refs_9_.refs_6_, ...), custom_call_target="tpu_custom_call" | custom-call | flops 3900000000 | bytes 14954528 | tf_op jit(solution)/shard_map/branch/pallas_call | solution.py:173
  162.1 11.7 %branch_back.1 = (bf16[1536,512]{1,0:T(8,128)(2,1)S(1)}, f32[1536,512]{1,0:T(8,128)S(1)}, f32[1536,512]{1,0:T(8,128)S(1)}, f32[1,2,512]{2,1,0:T(2,128)S(1)}) custom-call(s32[8]{0:T(128)S(1)} %broadcast_18_refs_0_.2.refs_0_, f32[1536,512]{1,0:T(8,128)S(1)} %get-tuple-element.109.refs_0_.refs_1_, f32[1536,512]{1,0:T(8,128)S(1)} %get-tuple-element.112.refs_2_, ...), custom_call_target="tpu_custom_call" | custom-call | flops 4499999744 | bytes 24399904 | tf_op jit(solution)/shard_map/branch_back/pallas_call | solution.py:173
  173.9 10.2 %branch_weight.1.refs_0_ = bf16[512,4608]{1,0:T(8,128)(2,1)S(1)} custom-call(s32[8]{0:T(128)S(1)} %broadcast_18_refs_0_.2.refs_0_, bf16[1536,512]{1,0:T(8,128)(2,1)S(1)} %get-tuple-element.114.refs_1_, bf16[512,1536]{1,0:T(8,128)(2,1)S(1)} %merged_turn.1.refs_2_), custom_call_target="tpu_custom_call" | custom-call | flops 3000000000 | bytes 7864352 | tf_op jit(solution)/shard_map/branch_weight/pallas_call | solution.py:173
  193.8 4.7 collective-permute-done.43
  200.4 5.7 %second_back.1 = (bf16[1536,512]{1,0:T(8,128)(2,1)S(1)}, f32[1536,512]{1,0:T(8,128)S(1)}, f32[1,2,512]{2,1,0:T(2,128)S(1)}) custom-call(bf16[512,4608]{1,0:T(8,128)(2,1)} %copy-done, f32[1536,512]{1,0:T(8,128)S(1)} %copy-done.8, f32[1536,512]{1,0:T(8,128)} %copy-done.3, f32[1536,512]{1,0:T(8,128)} %copy-done.1, ...), custom_call_target="tpu_custom_call" | custom-call | flops 1500000000 | bytes 16011264 | tf_op jit(solution)/shard_map/second_back/pallas_call | solution.py:173
  227.6 8.7 %collective-permute-done.54 = bf16[64,1024]{1,0:T(8,128)(2,1)S(1)} collective-permute-done((bf16[64,1024]{1,0:T(8,128)(2,1)S(1)}, bf16[64,1024]{1,0:T(8,128)(2,1)S(1)}, u32[]{:S(2)}, u32[]{:S(2)}) %collective-permute-start.54) | collective-permute-done | bytes 131104 | tf_op jit(solution)/shard_map/ppermute | solution.py:62
  270.5 11.6 %trunk_weight.1 = (bf16[64,4608]{1,0:T(8,128)(2,1)S(1)}, bf16[64,4608]{1,0:T(8,128)(2,1)S(1)}, bf16[64,4608]{1,0:T(8,128)(2,1)S(1)}, bf16[64,4608]{1,0:T(8,128)(...) custom-call(bf16[64,1024]{1,0:T(8,128)(2,1)S(1)} %collective-permute, ...), custom_call_target="tpu_custom_call" | custom-call | flops 1800000000 | bytes 9838848 | tf_op jit(solution)/shard_map/trunk_weight/pallas_call | solution.py:173
  285.7 4.7 input.1
  290.4 5.4 %collective-permute-done.86.refs_2_ = bf16[64,4608]{1,0:T(8,128)(2,1)S(1)} collective-permute-done((bf16[64,4608]{1,0:T(8,128)(2,1)S(1)}, bf16[64,4608]{1,0:T(8,128)(2,1)S(1)}, u32[]{:S(2)}, u32[]{:S(2)}) %collective-permute-start.86) | collective-permute-done | bytes 589856 | tf_op jit(solution)/shard_map/ppermute | solution.py:62
  295.8 7.1 %collective-permute-done.87.refs_3_ = bf16[64,4608]{1,0:T(8,128)(2,1)S(1)} collective-permute-done((bf16[64,4608]{1,0:T(8,128)(2,1)S(1)}, bf16[64,4608]{1,0:T(8,128)(2,1)S(1)}, u32[]{:S(2)}, u32[]{:S(2)}) %collective-permute-start.87) | collective-permute-done | bytes 589856 | tf_op jit(solution)/shard_map/ppermute | solution.py:62
  302.8 13.3 %collective-permute-done.88.refs_4_ = bf16[64,4608]{1,0:T(8,128)(2,1)S(1)} collective-permute-done((bf16[64,4608]{1,0:T(8,128)(2,1)S(1)}, bf16[64,4608]{1,0:T(8,128)(2,1)S(1)}, u32[]{:S(2)}, u32[]{:S(2)}) %collective-permute-start.88) | collective-permute-done | bytes 589856 | tf_op jit(solution)/shard_map/ppermute | solution.py:62
  322.4 15.0 %pair_new.1 = (f32[64,512]{1,0:T(8,128)}, f32[64,512]{1,0:T(8,128)}) custom-call(bf16[64,1024]{1,0:T(8,128)(2,1)S(1)} %get-tuple-element.133.refs_0_, bf16[64,1024]{1,0:T(8,128)(2,1)S(1)} %collective-permute-done.56.refs_0_.refs_1_, bf16[64,1024]{1,0:T(8,128)(2,1)S(1)} %collective-permute-done.57.refs_1_.refs_2_, ...), custom_call_target="tpu_custom_call" | custom-call | flops 5400000000 | bytes 1835008 | tf_op jit(solution)/shard_map/pair_new/pallas_call | solution.py:173
  337.4 8.5 %collective-permute-done.90.refs_4_ = bf16[64,4608]{1,0:T(8,128)(2,1)S(1)} collective-permute-done((bf16[64,4608]{1,0:T(8,128)(2,1)S(1)}, bf16[64,4608]{1,0:T(8,128)(2,1)S(1)}, u32[]{:S(2)}, u32[]{:S(2)}) %collective-permute-start.90) | collective-permute-done | bytes 589856 | tf_op jit(solution)/shard_map/ppermute | solution.py:62
  346.0 12.1 %collective-permute-done.91.refs_5_ = bf16[64,4608]{1,0:T(8,128)(2,1)S(1)} collective-permute-done((bf16[64,4608]{1,0:T(8,128)(2,1)S(1)}, bf16[64,4608]{1,0:T(8,128)(2,1)S(1)}, u32[]{:S(2)}, u32[]{:S(2)}) %collective-permute-start.91) | collective-permute-done | bytes 589856 | tf_op jit(solution)/shard_map/ppermute | solution.py:62
  451.4 10.7 %conv_new.1.refs_0_ = f32[9,64,512]{2,1,0:T(8,128)} custom-call(s32[64]{0:T(128)S(1)} %concatenate.5.refs_2_.refs_0_.refs_1_.refs_7_, f32[64,512]{1,0:T(8,128)S(1)} %copy-done.28, f32[64,512]{1,0:T(8,128)S(1)} %collective-permute-done.79.refs_2_.refs_0_, f32[64,512]{1,0:T(8,128)S(1)} %collective-permute-done.80.refs_3_.refs_1_, ...), custom_call_target="tpu_custom_call" | custom-call | flops 3300000000 | bytes 4587776 | tf_op jit(solution)/shard_map/conv_new/pallas_call | solution.py:173
  463.5 9.1 %trunk_new.1 = f32[9,64,128]{2,1,0:T(8,128)} custom-call(f32[9,64,512]{2,1,0:T(8,128)S(1)} %copy-done.51, s32[64]{0:T(128)S(1)} %constant_dynamic-update-slice_fusion.refs_1_, f32[128,512]{1,0:T(8,128)S(1)} %bitcast.41, f32[128,512]{1,0:T(8,128)S(1)} %collective-permute-done.99.refs_3_, f32[128,512]{1,0:T(8,128)} %collective-permute-done.100.refs_4_, ...), custom_call_target="tpu_custom_call" | custom-call | flops 3300000000 | bytes 2818304 | tf_op jit(solution)/shard_map/trunk_new/pallas_call | solution.py:173
  (384 shorter events, 263.8 us)
Async XLA Ops:
  7.2 117.1 %all-gather.2.cloned.1.call-start = ((), (), s32[]{:S(2)}) async-start(), calls=%async_computation.4 | async-start | bytes 5308416 | tf_op jit(solution)/shard_map/all_gather | solution.py:973
  9.4 356.9 %reduce-scatter.2.cloned.1.call-start = ((), (), s32[]{:S(2)}) async-start(), calls=%async_computation.5 | async-start | bytes 5308416 | tf_op jit(solution)/shard_map/reduce_scatter | solution.py:108
  26.4 19.0 %collective-permute-start.6 = (bf16[1536,128]{1,0:T(8,128)(2,1)S(1)}, bf16[1536,128]{1,0:T(8,128)(2,1)S(1)}, u32[]{:S(2)}, u32[]{:S(2)}) collective-permute-start(bf16[1536,128]{1,0:T(8,128)(2,1)S(1)} %bitcast.36), channel_id=1, source_target_pairs={{0,1},{1,0},{2,3},{3,2},{4,5},{5,4},{6,7},{7,6},{8,9},{9,8},{10,11... | collective-permute-start | bytes 1179656 | tf_op jit(solution)/shard_map/ppermute | solution.py:120
  26.5 25.7 %collective-permute-start.8 = (bf16[1536,128]{1,0:T(8,128)(2,1)S(1)}, bf16[1536,128]{1,0:T(8,128)(2,1)S(1)}, u32[]{:S(2)}, u32[]{:S(2)}) collective-permute-start(bf16[1536,128]{1,0:T(8,128)(2,1)S(1)} %collective-permute-done.7.refs_5_.refs_2_), channel_id=1, source_target_pairs={{0,1},{1,0},{2,3},{3,2},{4,5},{5,4},{6,7},{7,6},{8,9},{9,8},{10,11... | collective-permute-start | bytes 1179656 | tf_op jit(solution)/shard_map/ppermute | solution.py:120
  30.1 15.3 %collective-permute-start.4 = (bf16[64,1024]{1,0:T(8,128)(2,1)}, bf16[64,1024]{1,0:T(8,128)(2,1)}, u32[]{:S(2)}, u32[]{:S(2)}) collective-permute-start(bf16[64,1024]{1,0:T(8,128)(2,1)} %collective-permute-done.3.refs_11_), channel_id=1, source_target_pairs={{0,4},{8,0},{16,8},{24,16},{28,24},{20,28},{12,20},{4,12},{1,5},{9... | collective-permute-start | bytes 393224 | tf_op jit(solution)/shard_map/ppermute | solution.py:57
  36.6 15.5 %collective-permute-start.15 = (bf16[64,1152]{1,0:T(8,128)(2,1)S(1)}, bf16[64,1152]{1,0:T(8,128)(2,1)S(1)}, u32[]{:S(2)}, u32[]{:S(2)}) collective-permute-start(bf16[64,1152]{1,0:T(8,128)(2,1)S(1)} %collective-permute-done.14.refs_15_), channel_id=1, source_target_pairs={{0,4},{8,0},{16,8},{24,16},{28,24},{20,28},{12,20},{4,12},{1,5},{9... | collective-permute-start | bytes 442376 | tf_op jit(solution)/shard_map/ppermute | solution.py:57
  36.6 15.5 %collective-permute-start.12 = (bf16[64,1152]{1,0:T(8,128)(2,1)S(1)}, bf16[64,1152]{1,0:T(8,128)(2,1)}, u32[]{:S(2)}, u32[]{:S(2)}) collective-permute-start(bf16[64,1152]{1,0:T(8,128)(2,1)S(1)} %collective-permute-done.11.refs_12_), channel_id=1, source_target_pairs={{0,8},{8,16},{16,24},{24,28},{28,20},{20,12},{12,4},{4,0},{1,9},{9... | collective-permute-start | bytes 442376 | tf_op jit(solution)/shard_map/ppermute | solution.py:55
  75.5 14.5 %collective-permute-start.20 = (bf16[1536,128]{1,0:T(8,128)(2,1)S(1)}, bf16[1536,128]{1,0:T(8,128)(2,1)S(1)}, u32[]{:S(2)}, u32[]{:S(2)}) collective-permute-start(bf16[1536,128]{1,0:T(8,128)(2,1)S(1)} %get-tuple-element.101.refs_1_), channel_id=1, source_target_pairs={{0,1},{1,0},{2,3},{3,2},{4,5},{5,4},{6,7},{7,6},{8,9},{9,8},{10,11... | collective-permute-start | bytes 1179656 | tf_op jit(solution)/shard_map/ppermute | solution.py:120
  219.4 21.8 %collective-permute-start.63 = (bf16[1536,128]{1,0:T(8,128)(2,1)S(1)}, bf16[1536,128]{1,0:T(8,128)(2,1)S(1)}, u32[]{:S(2)}, u32[]{:S(2)}) collective-permute-start(bf16[1536,128]{1,0:T(8,128)(2,1)S(1)} %get-tuple-element.135), channel_id=1, source_target_pairs={{0,2},{1,3},{2,0},{3,1},{4,6},{5,7},{6,4},{7,5},{8,10},{9,11},{10,... | collective-permute-start | bytes 1179656 | tf_op jit(solution)/shard_map/ppermute | solution.py:120
  227.2 15.0 %collective-permute-start.64 = (bf16[1536,128]{1,0:T(8,128)(2,1)S(1)}, bf16[1536,128]{1,0:T(8,128)(2,1)S(1)}, u32[]{:S(2)}, u32[]{:S(2)}) collective-permute-start(bf16[1536,128]{1,0:T(8,128)(2,1)S(1)} %get-tuple-element.136), channel_id=1, source_target_pairs={{0,3},{1,2},{2,1},{3,0},{4,7},{5,6},{6,5},{7,4},{8,11},{9,10},{10,... | collective-permute-start | bytes 1179656 | tf_op jit(solution)/shard_map/ppermute | solution.py:120
  282.5 20.3 %collective-permute-start.87 = (bf16[64,4608]{1,0:T(8,128)(2,1)S(1)}, bf16[64,4608]{1,0:T(8,128)(2,1)S(1)}, u32[]{:S(2)}, u32[]{:S(2)}) collective-permute-start(bf16[64,4608]{1,0:T(8,128)(2,1)S(1)} %get-tuple-element.158), channel_id=1, source_target_pairs={{0,8},{4,12},{8,0},{12,4},{16,24},{20,28},{24,16},{28,20},{1,9},{5... | collective-permute-start | bytes 1769480 | tf_op jit(solution)/shard_map/ppermute | solution.py:62
  282.5 33.6 %collective-permute-start.88 = (bf16[64,4608]{1,0:T(8,128)(2,1)S(1)}, bf16[64,4608]{1,0:T(8,128)(2,1)S(1)}, u32[]{:S(2)}, u32[]{:S(2)}) collective-permute-start(bf16[64,4608]{1,0:T(8,128)(2,1)S(1)} %get-tuple-element.159), channel_id=1, source_target_pairs={{0,12},{4,8},{8,4},{12,0},{16,28},{20,24},{24,20},{28,16},{1,13},{... | collective-permute-start | bytes 1769480 | tf_op jit(solution)/shard_map/ppermute | solution.py:62
  316.4 21.0 %collective-permute-start.89 = (bf16[64,4608]{1,0:T(8,128)(2,1)S(1)}, bf16[64,4608]{1,0:T(8,128)(2,1)S(1)}, u32[]{:S(2)}, u32[]{:S(2)}) collective-permute-start(bf16[64,4608]{1,0:T(8,128)(2,1)S(1)} %get-tuple-element.163), channel_id=1, source_target_pairs={{0,4},{4,0},{8,12},{12,8},{16,20},{20,16},{24,28},{28,24},{1,5},{5... | collective-permute-start | bytes 1769480 | tf_op jit(solution)/shard_map/ppermute | solution.py:62
  317.1 28.9 %collective-permute-start.90 = (bf16[64,4608]{1,0:T(8,128)(2,1)S(1)}, bf16[64,4608]{1,0:T(8,128)(2,1)S(1)}, u32[]{:S(2)}, u32[]{:S(2)}) collective-permute-start(bf16[64,4608]{1,0:T(8,128)(2,1)S(1)} %get-tuple-element.164), channel_id=1, source_target_pairs={{0,8},{4,12},{8,0},{12,4},{16,24},{20,28},{24,16},{28,20},{1,9},{5... | collective-permute-start | bytes 1769480 | tf_op jit(solution)/shard_map/ppermute | solution.py:62
  317.4 40.7 %collective-permute-start.91 = (bf16[64,4608]{1,0:T(8,128)(2,1)S(1)}, bf16[64,4608]{1,0:T(8,128)(2,1)S(1)}, u32[]{:S(2)}, u32[]{:S(2)}) collective-permute-start(bf16[64,4608]{1,0:T(8,128)(2,1)S(1)} %get-tuple-element.165), channel_id=1, source_target_pairs={{0,12},{4,8},{8,4},{12,0},{16,28},{20,24},{24,20},{28,16},{1,13},{... | collective-permute-start | bytes 1769480 | tf_op jit(solution)/shard_map/ppermute | solution.py:62
  320.0 38.0 %collective-permute-start.92 = (bf16[64,4608]{1,0:T(8,128)(2,1)S(1)}, bf16[64,4608]{1,0:T(8,128)(2,1)S(1)}, u32[]{:S(2)}, u32[]{:S(2)}) collective-permute-start(bf16[64,4608]{1,0:T(8,128)(2,1)S(1)} %get-tuple-element.166), channel_id=1, source_target_pairs={{0,16},{4,20},{8,24},{12,28},{16,0},{20,4},{24,8},{28,12},{1,17},{... | collective-permute-start | bytes 1769480 | tf_op jit(solution)/shard_map/ppermute | solution.py:62
  362.4 22.7 %all-to-all-start = ((f32[32,16,128]{2,1,0:T(8,128)}), f32[32,16,128]{2,1,0:T(8,128)}, u32[]{:S(2)}, u32[]{:S(2)}) async-start(f32[32,16,128]{2,1,0:T(8,128)} %get-tuple-element.167), calls=%async_computation.1 | async-start | bytes 524288 | tf_op jit(solution)/shard_map/all_to_all | solution.py:1308
  402.2 23.4 %all-to-all-start.1 = ((f32[8,16,512]{2,1,0:T(8,128)}), f32[8,16,512]{2,1,0:T(8,128)S(1)}, u32[]{:S(2)}, u32[]{:S(2)}) async-start(f32[8,16,512]{2,1,0:T(8,128)} %get-tuple-element.171), calls=%async_computation.2 | async-start | bytes 524288 | tf_op jit(solution)/shard_map/all_to_all | solution.py:1335
  406.1 24.2 %collective-permute-start.70 = (bf16[1536,128]{1,0:T(8,128)(2,1)}, bf16[1536,128]{1,0:T(8,128)(2,1)}, u32[]{:S(2)}, u32[]{:S(2)}) collective-permute-start(bf16[1536,128]{1,0:T(8,128)(2,1)} %get-tuple-element.142), channel_id=1, source_target_pairs={{0,1},{1,0},{2,3},{3,2},{4,5},{5,4},{6,7},{7,6},{8,9},{9,8},{10,11... | collective-permute-start | bytes 1179656 | tf_op jit(solution)/shard_map/ppermute | solution.py:120
  411.3 14.3 %collective-permute-start.93 = (bf16[576,128]{1,0:T(8,128)(2,1)S(1)}, bf16[576,128]{1,0:T(8,128)(2,1)S(1)}, u32[]{:S(2)}, u32[]{:S(2)}) collective-permute-start(bf16[576,128]{1,0:T(8,128)(2,1)S(1)} %get-tuple-element.169.refs_6_), channel_id=1, source_target_pairs={{0,1},{1,0},{2,3},{3,2},{4,5},{5,4},{6,7},{7,6},{8,9},{9,8},{10,11... | collective-permute-start | bytes 442376 | tf_op jit(solution)/shard_map/ppermute | solution.py:120
  421.6 15.5 %collective-permute-start.69 = (bf16[1536,128]{1,0:T(8,128)(2,1)}, bf16[1536,128]{1,0:T(8,128)(2,1)}, u32[]{:S(2)}, u32[]{:S(2)}) collective-permute-start(bf16[1536,128]{1,0:T(8,128)(2,1)} %get-tuple-element.140), channel_id=1, source_target_pairs={{0,1},{1,0},{2,3},{3,2},{4,5},{5,4},{6,7},{7,6},{8,9},{9,8},{10,11... | collective-permute-start | bytes 1179656 | tf_op jit(solution)/shard_map/ppermute | solution.py:120
  433.6 14.7 %collective-permute-start.83 = (f32[64,512]{1,0:T(8,128)}, f32[64,512]{1,0:T(8,128)}, u32[]{:S(2)}, u32[]{:S(2)}) collective-permute-start(f32[64,512]{1,0:T(8,128)} %copy-done.25), channel_id=1, source_target_pairs={{0,4},{4,0},{8,12},{12,8},{16,20},{20,16},{24,28},{28,24},{1,5},{5... | collective-permute-start | bytes 393224 | tf_op jit(solution)/shard_map/ppermute | solution.py:62
  447.5 14.7 %collective-permute-start.99 = (f32[128,512]{1,0:T(8,128)S(1)}, f32[128,512]{1,0:T(8,128)S(1)}, u32[]{:S(2)}, u32[]{:S(2)}) collective-permute-start(f32[128,512]{1,0:T(8,128)S(1)} %bitcast.40), channel_id=1, source_target_pairs={{0,1},{1,0},{2,3},{3,2},{4,5},{5,4},{6,7},{7,6},{8,9},{9,8},{10,11... | collective-permute-start | bytes 786440 | tf_op jit(solution)/shard_map/ppermute | solution.py:120
  448.3 13.9 %collective-permute-start.101 = (f32[128,512]{1,0:T(8,128)}, f32[128,512]{1,0:T(8,128)S(1)}, u32[]{:S(2)}, u32[]{:S(2)}) collective-permute-start(f32[128,512]{1,0:T(8,128)} %collective-permute-done.100.refs_4_), channel_id=1, source_target_pairs={{0,1},{1,0},{2,3},{3,2},{4,5},{5,4},{6,7},{7,6},{8,9},{9,8},{10,11... | collective-permute-start | bytes 786440 | tf_op jit(solution)/shard_map/ppermute | solution.py:120
  (147 other events, 1363.8 us)
Sparse Core Ops, SparseCore 0:
  10.8 91.2 all-gather.1
  186.4 107.9 reduce-scatter.1
